TPU v7x, 128 devices: a whole 4x4x4 slice. The times are simulated.
128 devices in a mesh: dp: 4 (over y_lo, core), ctx: 32 (over y_hi, x, z).
Axes of the slice: x: 4, y: 4 (y_hi: 2, y_lo: 2; y = y_hi * 2 + y_lo), z: 4, core: 2. Of those that a mesh axis runs over, the one named last changes fastest.
Arguments:
- hidden: bfloat16 [4, 8192, 4096], P('dp', 'ctx'), may hold values from -6 to 6
- projected: bfloat16 [3, 4, 8192, 2048], P(None, 'dp', 'ctx'), may hold values from -72 to 72, as said below
- output_gradient: bfloat16 [4, 8192, 4096], P('dp', 'ctx'), may hold values from -6 to 6
- output_weight: bfloat16 [2048, 4096], replicated, may hold values from -0.125 to 0.125
- adapter_down_weight: bfloat16 [3, 8, 4096], replicated, may hold values from -0.09375 to 0.09375
- adapter_up_weight: bfloat16 [3, 8, 2048], replicated, may hold values from -2 to 2
- output_down_weight: bfloat16 [8, 2048], replicated, may hold values from -0.125 to 0.125
- output_up_weight: bfloat16 [8, 4096], replicated, may hold values from -2 to 2
Outputs:
- input_gradient: bfloat16 [4, 8192, 4096], P('dp', 'ctx')
- grad_down: bfloat16 [3, 8, 4096], replicated
- grad_up: bfloat16 [3, 8, 2048], replicated
- grad_down_o: bfloat16 [8, 2048], replicated
- grad_up_o: bfloat16 [8, 4096], replicated
Inputs may be any that keep to these rules, and one draw needn't show every extreme that they name: `projected`: queries, keys and values, heads side by side along the last dimension.
All inputs are finite; a program needn't handle non-finite values.
Results may differ from a plain program's by a relative error of at most 0.0085.
Values may be sent and summed in bfloat16 or wider, within the bound.
A program may use at most 128 MiB of HBM per device.

v0:
```python
import math

import jax
import jax.numpy as jnp
from jax import lax
from jax.sharding import PartitionSpec as P

HEAD_WIDTH = 128


ADAPTER_SCALE = 2.0


def passed_along(x, axis, by):
    peers = lax.axis_size(axis)
    return lax.ppermute(x, axis, [(i, (i + by) % peers) for i in range(peers)])


def attend(queries, key_rows, values, attention_gradient, visible):
    score_scale = 1.0 / math.sqrt(queries.shape[-1])
    scores = (
        jnp.einsum("qhe,khe->hqk", queries, key_rows, preferred_element_type=jnp.float32)
        * score_scale
    )
    scores = jnp.where(visible[None], scores, -jnp.inf)
    row_max = jnp.max(scores, axis=-1, keepdims=True)
    raised = jnp.exp(scores - row_max)
    attn_probs = raised / jnp.sum(raised, axis=-1, keepdims=True)
    probs_low = attn_probs.astype(jnp.bfloat16)
    attended = jnp.einsum(
        "hqk,khe->qhe", probs_low, values, preferred_element_type=jnp.float32
    ).astype(jnp.bfloat16)
    d_probs = jnp.einsum(
        "qhe,khe->hqk", attention_gradient, values, preferred_element_type=jnp.float32
    )
    row_dot = jnp.sum(attn_probs * d_probs, axis=-1, keepdims=True)
    d_scores = (attn_probs * (d_probs - row_dot)).astype(jnp.bfloat16)
    query_gradient = (
        jnp.einsum("hqk,khe->qhe", d_scores, key_rows, preferred_element_type=jnp.float32)
        * score_scale
    )
    key_gradient = (
        jnp.einsum("hqk,qhe->khe", d_scores, queries, preferred_element_type=jnp.float32)
        * score_scale
    )
    value_gradient = jnp.einsum(
        "hqk,qhe->khe", probs_low, attention_gradient, preferred_element_type=jnp.float32
    )
    return (attended, query_gradient, key_gradient, value_gradient)


def split_heads(matrix):
    return matrix.reshape(matrix.shape[0], -1, HEAD_WIDTH)


def join_heads(tensor):
    return tensor.reshape(tensor.shape[0], -1)


def take_half(matrix, offset, half_width, axis_index):
    return lax.dynamic_slice_in_dim(matrix, offset, half_width, axis_index)


def place_halves(first_part, pair_part, first_start, pair_start):
    whole = jnp.zeros((first_part.shape[0], 2 * first_part.shape[1]), first_part.dtype)
    whole = lax.dynamic_update_slice_in_dim(whole, first_part, first_start, 1)
    return lax.dynamic_update_slice_in_dim(whole, pair_part, pair_start, 1)


def adapter_pieces(
    weight_gradients, adapter_down_weight, adapter_up_weight, hidden_token_rows, scale_factor
):
    thin_input = jnp.einsum(
        "yz,swz->syw", hidden_token_rows, adapter_down_weight, preferred_element_type=jnp.float32
    ).astype(jnp.bfloat16)
    thin_gradient = jnp.einsum(
        "zmq,zlq->zml", weight_gradients, adapter_up_weight, preferred_element_type=jnp.float32
    ).astype(jnp.bfloat16)
    piece_up_weight = (
        jnp.einsum("ctr,cth->crh", thin_input, weight_gradients, preferred_element_type=jnp.float32)
        * scale_factor
    )
    piece_down_weight = (
        jnp.einsum(
            "ctr,td->crd", thin_gradient, hidden_token_rows, preferred_element_type=jnp.float32
        )
        * scale_factor
    )
    inner_total_sum = jnp.einsum(
        "wgs,wsf->gf", thin_gradient, adapter_down_weight, preferred_element_type=jnp.float32
    )
    return (piece_up_weight, piece_down_weight, inner_total_sum)


def per_device(
    hidden,
    projected,
    output_gradient,
    output_weight,
    adapter_down_weight,
    adapter_up_weight,
    output_down_weight,
    output_up_weight,
):
    hidden_token_rows = hidden[0]
    cotangent = output_gradient[0]
    queries = projected[0, 0]
    key_value = projected[1:, 0]
    token_count = queries.shape[0]
    half_width = queries.shape[1] // 2
    parity = lax.axis_index("ctx") % 2
    first_start = parity * half_width
    pair_start = (1 - parity) * half_width
    scale_factor = ADAPTER_SCALE / (token_count * lax.axis_size("ctx") * lax.axis_size("dp"))
    output_thin_gradient = jnp.einsum(
        "td,rd->tr", cotangent, output_up_weight, preferred_element_type=jnp.float32
    ).astype(jnp.bfloat16)
    attention_gradient = (
        jnp.einsum("td,hd->th", cotangent, output_weight, preferred_element_type=jnp.float32)
        + ADAPTER_SCALE
        * jnp.dot(output_thin_gradient, output_down_weight, preferred_element_type=jnp.float32)
    ).astype(jnp.bfloat16)
    own_first = take_half(key_value, first_start, half_width, 2)
    own_pair = take_half(key_value, pair_start, half_width, 2)
    arrived = passed_along(key_value, "ctx", 1)
    remote = take_half(arrived, pair_start, half_width, 2)
    position = jnp.arange(token_count)
    causal = position[:, None] >= position[None, :]
    first_out = attend(
        split_heads(take_half(queries, first_start, half_width, 1)),
        split_heads(own_first[0]),
        split_heads(own_first[1]),
        split_heads(take_half(attention_gradient, first_start, half_width, 1)),
        causal,
    )
    visible = jnp.concatenate([jnp.ones((token_count, token_count), jnp.bool_), causal], axis=1)
    pair_keys = jnp.concatenate([remote, own_pair], axis=1)
    pair_out = attend(
        split_heads(take_half(queries, pair_start, half_width, 1)),
        split_heads(pair_keys[0]),
        split_heads(pair_keys[1]),
        split_heads(take_half(attention_gradient, pair_start, half_width, 1)),
        visible,
    )
    attended = place_halves(
        join_heads(first_out[0]), join_heads(pair_out[0]), first_start, pair_start
    )
    query_gradient = place_halves(
        join_heads(first_out[1]), join_heads(pair_out[1]), first_start, pair_start
    ).astype(jnp.bfloat16)
    low_o = jnp.einsum(
        "th,rh->tr", attended, output_down_weight, preferred_element_type=jnp.float32
    ).astype(jnp.bfloat16)
    part_up_o = (
        jnp.einsum("tr,td->rd", low_o, cotangent, preferred_element_type=jnp.float32) * scale_factor
    )
    part_down_o = (
        jnp.einsum("tr,th->rh", output_thin_gradient, attended, preferred_element_type=jnp.float32)
        * scale_factor
    )
    remote_grads = jnp.stack(
        [join_heads(pair_out[2][:token_count]), join_heads(pair_out[3][:token_count])]
    ).astype(jnp.bfloat16)
    returned = passed_along(remote_grads, "ctx", -1).astype(jnp.float32)
    key_gradient = place_halves(
        join_heads(first_out[2]) + returned[0],
        join_heads(pair_out[2][token_count:]),
        first_start,
        pair_start,
    ).astype(jnp.bfloat16)
    value_gradient = place_halves(
        join_heads(first_out[3]) + returned[1],
        join_heads(pair_out[3][token_count:]),
        first_start,
        pair_start,
    ).astype(jnp.bfloat16)
    piece_up_weight, piece_down_weight, inner_total_sum = adapter_pieces(
        jnp.stack([query_gradient, key_gradient, value_gradient]),
        adapter_down_weight,
        adapter_up_weight,
        hidden_token_rows,
        scale_factor,
    )
    grad_up, grad_down, grad_up_o, grad_down_o = lax.psum(
        (piece_up_weight, piece_down_weight, part_up_o, part_down_o), ("dp", "ctx")
    )
    input_gradient = (ADAPTER_SCALE * inner_total_sum).astype(jnp.bfloat16)
    return (
        input_gradient[None],
        grad_down.astype(jnp.bfloat16),
        grad_up.astype(jnp.bfloat16),
        grad_down_o.astype(jnp.bfloat16),
        grad_up_o.astype(jnp.bfloat16),
    )


def solution(mesh):
    in_specs = (
        P("dp", "ctx", None),
        P(None, "dp", "ctx", None),
        P("dp", "ctx", None),
        P(),
        P(),
        P(),
        P(),
        P(),
    )
    out_specs = (P("dp", "ctx", None), P(), P(), P(), P())
    return jax.shard_map(
        per_device, mesh=mesh, in_specs=in_specs, out_specs=out_specs, check_vma=False
    )
```

profile of v0, /device:TPU:1, one launch (start us, length us, event | category | flops | bytes accessed | tf_op | source)
XLA Modules:
  0.0 200.7 jit_solution(1329883331311712115)
XLA Ops:
  0.6 3.3 %slice.40 = bf16[2,1,256,2048]{3,2,1,0:T(8,128)(2,1)} slice(bf16[3,1,256,2048]{3,2,1,0:T(8,128)(2,1)} %param.9), slice={[1:3], [0:1], [0:256], [0:2048]} | slice | bytes 4194304 | tf_op jit(solution)/shard_map/slice | solution.py:108
  4.0 3.9 %copy.71 = bf16[2,1,256,2048]{2,3,1,0:T(8,128)(2,1)} copy(bf16[2,1,256,2048]{3,2,1,0:T(8,128)(2,1)} %slice.40) | data formatting | bytes 4194304
  7.9 2.5 %collective-permute-start = (bf16[2,256,2048]{1,2,0:T(8,128)(2,1)}, bf16[2,256,2048]{1,2,0:T(8,128)(2,1)}, u32[]{:S(2)}, u32[]{:S(2)}) collective-permute-start(bf16[2,256,2048]{1,2,0:T(8,128)(2,1)} %bitcast.122), channel_id=1, source_target_pairs={{0,1},{1,2},{2,3},{3,4},{4,5},{5,6},{6,7},{7,8},{8,9},{9,10},{10,1... | collective-permute-start | bytes 6291464 | tf_op jit(solution)/shard_map/ppermute | solution.py:16
  11.5 2.1 %copy.74 = bf16[1,1,256,1024]{2,3,1,0:T(8,128)(2,1)} copy(bf16[1,1,256,1024]{3,2,1,0:T(8,128)(2,1)} %get-tuple-element.17) | data formatting | bytes 1048576
  13.8 2.3 %constant_dynamic-slice_fusion.6 = (bf16[1,1,256,1024]{2,3,1,0:T(8,128)(2,1)}, bf16[1,1,256,1024]{2,3,1,0:T(8,128)(2,1)}) fusion(bf16[2,1,256,2048]{2,3,1,0:T(8,128)(2,1)} %copy.71, s32[]{:T(128)S(6)} %add.46, s32[]{:T(128)S(6)} %select_n.20), kind=kLoop, calls=%fused_computation.89 | loop fusion | bytes 2097160 | tf_op jit(solution)/shard_map/slice | solution.py:132
  17.0 9.5 %fusion.14 = f32[256,2048]{1,0:T(8,128)} fusion(bf16[2048,4096]{1,0:T(8,128)(2,1)} %param.11, bf16[1,256,4096]{2,1,0:T(8,128)(2,1)S(1)} %copy-done), kind=kOutput, calls=%fused_computation.27 | convolution fusion | flops 4294967296 | bytes 20971520 | tf_op jit(solution)/shard_map/td,hd->th/dot_general | solution.py:119
  26.4 2.1 %fusion.7 = bf16[256,2048]{1,0:T(8,128)(2,1)S(1)} fusion(f32[256,2048]{1,0:T(8,128)} %fusion.14, bf16[256,8]{0,1:T(8,128)(2,1)S(1)} %fusion.25, bf16[8,2048]{1,0:T(8,128)(2,1)S(1)} %copy-done.19), kind=kOutput, calls=%fused_computation.16 | convolution fusion | flops 9961472 | bytes 3182592 | tf_op jit(solution)/shard_map/dot_general | solution.py:121
  30.4 3.3 %fusion.55 = (f32[8,256]{1,0:T(8,128)S(1)}, f32[8,256,256]{1,2,0:T(8,128)}) fusion(pred[256,256]{0,1:T(8,128)(4,1)S(1)} %iota_compare_fusion, bf16[256,8,128]{0,2,1:T(8,128)(2,1)S(1)} %bitcast.128, bf16[256,8,128]{0,2,1:T(8,128)(2,1)} %bitcast.136), kind=kOutput, calls=%fused_computation.98 | convolution fusion | flops 136315136 | bytes 3219456 | tf_op jit(solution)/shard_map/sub | solution.py:27
  33.7 2.4 %multiply_reduce_fusion.1 = (f32[8,256]{1,0:T(8,128)S(1)}, f32[8,256,256]{1,2,0:T(8,128)S(1)}) fusion(f32[8,256,256]{1,2,0:T(8,128)} %get-tuple-element.22, f32[8,256]{1,0:T(8,128)S(1)} %get-tuple-element.21, bf16[256,8,128]{0,2,1:T(8,128)(2,1)S(1)} %bitcast.148, bf16[256,8,128]{0,2,1:T(8,128)(2,1)} %bitcast.151), kind=kOutput, calls=%fused_computation.34 | convolution fusion | flops 135788544 | bytes 5259264 | tf_op jit(solution)/shard_map/qhe,khe->hqk/dot_general | solution.py:33
  42.4 2.5 %convolution_multiply_fusion.5 = f32[8,128,256]{2,1,0:T(8,128)} fusion(bf16[256,8,128]{0,2,1:T(8,128)(2,1)} %bitcast.129, bf16[8,256,256]{1,2,0:T(8,128)(2,1)S(1)} %multiply_convert_fusion.1), kind=kOutput, calls=%fused_computation.40 | convolution fusion | flops 134479872 | bytes 2621440 | tf_op jit(solution)/shard_map/hqk,qhe->khe/dot_general | solution.py:43
  44.9 2.5 %copy.53 = f32[256,1024]{1,0:T(8,128)} copy(f32[256,1024]{0,1:T(8,128)} %bitcast.125) | data formatting | bytes 2097152 | tf_op jit(solution)/shard_map/reshape | solution.py:57
  47.4 2.3 %fusion.41 = f32[8,128,256]{2,1,0:T(8,128)S(1)} fusion(bf16[256,8,128]{0,2,1:T(8,128)(2,1)} %bitcast.147, f32[8,256,256]{1,2,0:T(8,128)} %get-tuple-element.22, f32[8,256]{1,0:T(8,128)S(1)} %get-tuple-element.21), kind=kOutput, calls=%fused_computation.72 | convolution fusion | flops 135266304 | bytes 3678208 | tf_op jit(solution)/shard_map/hqk,qhe->khe/dot_general | solution.py:46
  51.1 2.1 %convolution_convert_fusion.1 = bf16[8,128,256]{2,1,0:T(8,128)(2,1)S(1)} fusion(bf16[256,8,128]{0,2,1:T(8,128)(2,1)} %bitcast.152, f32[8,256,256]{1,2,0:T(8,128)} %get-tuple-element.22, f32[8,256]{1,0:T(8,128)S(1)} %get-tuple-element.21), kind=kOutput, calls=%fused_computation.44 | convolution fusion | flops 135528448 | bytes 3153920 | tf_op jit(solution)/shard_map/hqk,khe->qhe/dot_general | solution.py:30
  55.4 7.5 %collective-permute-done = bf16[2,256,2048]{1,2,0:T(8,128)(2,1)} collective-permute-done((bf16[2,256,2048]{1,2,0:T(8,128)(2,1)}, bf16[2,256,2048]{1,2,0:T(8,128)(2,1)}, u32[]{:S(2)}, u32[]{:S(2)}) %collective-permute-start) | collective-permute-done | bytes 2097184 | tf_op jit(solution)/shard_map/ppermute | solution.py:16
  65.8 4.9 %fusion.56 = (f32[8,256]{1,0:T(8,128)S(1)}, f32[8,256,512]{2,1,0:T(8,128)}) fusion(pred[256,512]{1,0:T(8,128)(4,1)S(1)} %concatenate.7.clone, bf16[256,8,128]{0,2,1:T(8,128)(2,1)} %bitcast.126, bf16[512,8,128]{0,2,1:T(8,128)(2,1)} %bitcast.123), kind=kOutput, calls=%fused_computation.99 | convolution fusion | flops 272630272 | bytes 5906432 | tf_op jit(solution)/shard_map/sub | solution.py:27
  70.7 4.4 %convolution_convert_fusion = bf16[8,128,256]{2,1,0:T(8,128)(2,1)} fusion(bf16[512,8,128]{0,2,1:T(8,128)(2,1)} %bitcast.143, f32[8,256,512]{2,1,0:T(8,128)} %get-tuple-element.24, f32[8,256]{1,0:T(8,128)S(1)} %get-tuple-element.23), kind=kOutput, calls=%fused_computation.43 | convolution fusion | flops 270794752 | bytes 5775360 | tf_op jit(solution)/shard_map/hqk,khe->qhe/dot_general | solution.py:30
  80.5 2.1 %copy.51 = bf16[1,256,1024]{2,1,0:T(8,128)(2,1)} copy(bf16[1,256,1024]{1,2,0:T(8,128)(2,1)} %bitcast.133) | data formatting | bytes 1048576 | tf_op jit(solution)/shard_map/stack;reshape | solution.py:161
  82.6 2.3 %fusion.54 = (bf16[256,8,128]{0,2,1:T(8,128)(2,1)}, bf16[256,8,128]{0,2,1:T(8,128)(2,1)}) fusion(bf16[512,8,128]{0,2,1:T(8,128)(2,1)} %convolution_bitcast_fusion.1), kind=kLoop, calls=%fused_computation.97 | loop fusion | bytes 2097152 | tf_op jit(solution)/shard_map/slice | solution.py:173
  87.0 2.3 %pad_maximum_fusion.6 = bf16[2,256,1024]{2,1,0:T(8,128)(2,1)} fusion(bf16[1,256,1024]{2,1,0:T(8,128)(2,1)} %copy.52, bf16[1,256,1024]{2,1,0:T(8,128)(2,1)} %copy.51), kind=kLoop, calls=%fused_computation.60 | loop fusion | flops 524288 | bytes 2097152 | tf_op jit(solution)/shard_map/stack | solution.py:161
  92.2 2.8 %convolution_multiply_fusion.6 = bf16[8,128,256]{2,1,0:T(8,128)(2,1)S(1)} fusion(bf16[512,8,128]{0,2,1:T(8,128)(2,1)} %bitcast.124, bf16[8,256,512]{2,1,0:T(8,128)(2,1)} %copy-done.1), kind=kOutput, calls=%fused_computation.41 | convolution fusion | flops 268959744 | bytes 3670016 | tf_op jit(solution)/shard_map/hqk,khe->qhe/dot_general | solution.py:39
  99.5 13.6 %collective-permute-done.1 = bf16[2,256,1024]{2,1,0:T(8,128)(2,1)} collective-permute-done((bf16[2,256,1024]{2,1,0:T(8,128)(2,1)}, bf16[2,256,1024]{2,1,0:T(8,128)(2,1)}, u32[]{:S(2)}, u32[]{:S(2)}) %collective-permute-start.1) | collective-permute-done | bytes 1048608 | tf_op jit(solution)/shard_map/ppermute | solution.py:16
  117.5 2.2 %fusion.21 = bf16[3,256,8]{1,2,0:T(8,128)(2,1)S(1)} fusion(bf16[3,8,2048]{2,1,0:T(8,128)(2,1)S(1)} %copy-done.22, bf16[1,256,2048]{2,1,0:T(8,128)(2,1)S(1)} %bitcast.138, bf16[1,256,2048]{2,1,0:T(8,128)(2,1)S(1)} %bitcast.141, bf16[1,256,2048]{2,1,0:T(8,128)(2,1)} %bitcast.86), kind=kOutput, calls=%fused_computation.47 | convolution fusion | flops 28317696 | bytes 3256320 | tf_op jit(solution)/shard_map/zmq,zlq->zml/dot_general | solution.py:76
  119.7 4.4 %convolution_multiply_fusion.3 = f32[3,8,2048]{2,1,0:T(8,128)S(1)} fusion(bf16[1,256,2048]{2,1,0:T(8,128)(2,1)} %bitcast.139, bf16[1,256,2048]{2,1,0:T(8,128)(2,1)} %bitcast.142, bf16[1,256,2048]{2,1,0:T(8,128)(2,1)} %bitcast.86, bf16[3,8,4096]{2,1,0:T(8,128)(2,1)S(1)} %copy-done.21, bf16[1,256,4096]{2,1,0:T(8,128)(2,1)} %param.8), kind=kOutput, calls=%fused_computation.17 | convolution fusion | flops 78698496 | bytes 5636096 | tf_op jit(solution)/shard_map/ctr,cth->crh/dot_general | solution.py:80
  128.2 72.6 %all-reduce.3 = (bf16[3,8,4096]{2,1,0:T(8,128)(2,1)}, bf16[3,8,2048]{2,1,0:T(8,128)(2,1)}, bf16[8,2048]{1,0:T(8,128)(2,1)}, bf16[8,4096]{1,0:T(8,128)(2,1)}) all-reduce(f32[3,8,4096]{2,1,0:T(8,128)S(1)} %convolution_multiply_fusion, f32[3,8,2048]{2,1,0:T(8,128)S(1)} %convolution_multiply_fusion.3, ...), channel_id=1, replica_groups=mesh['dp'=4,'ctx'=32] {'dp','ctx'}, use_global_device_ids=true, to_apply=%region_6.7 | all-reduce | flops 196608 | bytes 1179648 | tf_op jit(solution)/shard_map/psum | solution.py:184
  (90 shorter events, 39.9 us)
Async XLA Ops:
  0.6 15.7 %copy-start = (bf16[1,256,4096]{2,1,0:T(8,128)(2,1)S(1)}, bf16[1,256,4096]{2,1,0:T(8,128)(2,1)}, u32[]{:S(2)}) copy-start(bf16[1,256,4096]{2,1,0:T(8,128)(2,1)} %param.10) | copy-start | bytes 6291460
  7.9 2.5 %slice-start = ((bf16[3,1,256,2048]{3,2,1,0:T(8,128)(2,1)}), bf16[1,1,256,2048]{3,2,1,0:T(8,128)(2,1)S(1)}, s32[]{:S(2)}) async-start(bf16[3,1,256,2048]{3,2,1,0:T(8,128)(2,1)} %param.9), calls=%async_computation | async-start | bytes 2097152 | tf_op jit(solution)/shard_map/slice | solution.py:107
  7.9 55.1 %collective-permute-start = (bf16[2,256,2048]{1,2,0:T(8,128)(2,1)}, bf16[2,256,2048]{1,2,0:T(8,128)(2,1)}, u32[]{:S(2)}, u32[]{:S(2)}) collective-permute-start(bf16[2,256,2048]{1,2,0:T(8,128)(2,1)} %bitcast.122), channel_id=1, source_target_pairs={{0,1},{1,2},{2,3},{3,4},{4,5},{5,6},{6,7},{7,8},{8,9},{9,10},{10,1... | collective-permute-start | bytes 6291464 | tf_op jit(solution)/shard_map/ppermute | solution.py:16
  11.5 4.6 %copy-start.11 = (bf16[1,1,256,1024]{3,2,1,0:T(8,128)(2,1)S(1)}, bf16[1,1,256,1024]{3,2,1,0:T(8,128)(2,1)}, u32[]{:S(2)}) copy-start(bf16[1,1,256,1024]{3,2,1,0:T(8,128)(2,1)} %get-tuple-element.18) | copy-start | bytes 1572868
  11.5 4.8 %copy-start.20 = (bf16[8,4096]{1,0:T(8,128)(2,1)S(1)}, bf16[8,4096]{1,0:T(8,128)(2,1)}, u32[]{:S(2)}) copy-start(bf16[8,4096]{1,0:T(8,128)(2,1)} %param.15) | copy-start | bytes 196612
  16.3 14.1 %copy-start.7 = (bf16[1,1,256,1024]{2,3,1,0:T(8,128)(2,1)}, bf16[1,1,256,1024]{2,3,1,0:T(8,128)(2,1)S(1)}, u32[]{:S(2)}) copy-start(bf16[1,1,256,1024]{2,3,1,0:T(8,128)(2,1)S(1)} %copy.73) | copy-start | bytes 1572868
  17.0 9.5 %copy-start.19 = (bf16[8,2048]{1,0:T(8,128)(2,1)S(1)}, bf16[8,2048]{1,0:T(8,128)(2,1)}, u32[]{:S(2)}) copy-start(bf16[8,2048]{1,0:T(8,128)(2,1)} %param.14) | copy-start | bytes 98308
  30.4 3.3 %copy-start.17 = (bf16[256,1024]{0,1:T(8,128)(2,1)S(1)}, bf16[256,1024]{0,1:T(8,128)(2,1)}, u32[]{:S(2)}) copy-start(bf16[256,1024]{0,1:T(8,128)(2,1)} %copy.38) | copy-start | bytes 1572868
  33.7 2.4 %copy-start.8 = (f32[8,256,256]{1,2,0:T(8,128)S(1)}, f32[8,256,256]{1,2,0:T(8,128)}, u32[]{:S(2)}) copy-start(f32[8,256,256]{1,2,0:T(8,128)} %get-tuple-element.22) | copy-start | bytes 6291460
  36.1 1.0 copy-start.12
  53.2 1.3 copy-start.9
  53.2 2.2 %copy-start.2 = (bf16[2,1,256,2048]{2,3,1,0:T(8,128)(2,1)S(1)}, bf16[2,1,256,2048]{2,3,1,0:T(8,128)(2,1)}, u32[]{:S(2)}) copy-start(bf16[2,1,256,2048]{2,3,1,0:T(8,128)(2,1)} %copy.71) | copy-start | bytes 6291460
  70.7 4.4 %copy-start.3 = (f32[8,256,512]{2,1,0:T(8,128)S(1)}, f32[8,256,512]{2,1,0:T(8,128)}, u32[]{:S(2)}) copy-start(f32[8,256,512]{2,1,0:T(8,128)} %get-tuple-element.24) | copy-start | bytes 12582916
  70.7 4.4 %copy-start.15 = (bf16[1,512,1024]{1,2,0:T(8,128)(2,1)S(1)}, bf16[1,512,1024]{1,2,0:T(8,128)(2,1)}, u32[]{:S(2)}) copy-start(bf16[1,512,1024]{1,2,0:T(8,128)(2,1)} %get-tuple-element.11) | copy-start | bytes 3145732
  70.7 4.4 %copy-start.16 = (bf16[256,1024]{0,1:T(8,128)(2,1)S(1)}, bf16[256,1024]{0,1:T(8,128)(2,1)}, u32[]{:S(2)}) copy-start(bf16[256,1024]{0,1:T(8,128)(2,1)} %copy.46) | copy-start | bytes 1572868
  78.9 1.7 copy-start.1
  87.0 3.5 %copy-start.18 = (bf16[8,128,256]{2,1,0:T(8,128)(2,1)S(1)}, bf16[8,128,256]{2,1,0:T(8,128)(2,1)}, u32[]{:S(2)}) copy-start(bf16[8,128,256]{2,1,0:T(8,128)(2,1)} %convolution_convert_fusion) | copy-start | bytes 1572868
  89.3 23.8 %collective-permute-start.1 = (bf16[2,256,1024]{2,1,0:T(8,128)(2,1)}, bf16[2,256,1024]{2,1,0:T(8,128)(2,1)}, u32[]{:S(2)}, u32[]{:S(2)}) collective-permute-start(bf16[2,256,1024]{2,1,0:T(8,128)(2,1)} %pad_maximum_fusion.6), channel_id=1, source_target_pairs={{0,31},{1,0},{2,1},{3,2},{4,3},{5,4},{6,5},{7,6},{8,7},{9,8},{10,9... | collective-permute-start | bytes 3145736 | tf_op jit(solution)/shard_map/ppermute | solution.py:16
  92.2 3.8 %copy-start.10 = (bf16[256,8,128]{0,2,1:T(8,128)(2,1)S(1)}, bf16[256,8,128]{0,2,1:T(8,128)(2,1)}, u32[]{:S(2)}) copy-start(bf16[256,8,128]{0,2,1:T(8,128)(2,1)} %get-tuple-element.13) | copy-start | bytes 1572868
  99.5 15.2 %copy-start.5 = (f32[256,1024]{1,0:T(8,128)S(1)}, f32[256,1024]{1,0:T(8,128)}, u32[]{:S(2)}) copy-start(f32[256,1024]{1,0:T(8,128)} %copy.53) | copy-start | bytes 3145732
  114.6 1.2 copy-start.4
  115.9 1.6 copy-start.22
  116.1 1.3 copy-start.14
  117.5 2.2 %copy-start.21 = (bf16[3,8,4096]{2,1,0:T(8,128)(2,1)S(1)}, bf16[3,8,4096]{2,1,0:T(8,128)(2,1)}, u32[]{:S(2)}) copy-start(bf16[3,8,4096]{2,1,0:T(8,128)(2,1)} %param.12) | copy-start | bytes 589828
  (2 other events, 2.0 us)
where the time goes:
time: 202 us; the launch traced here: 201 us
  blocking collectives  72.6 us (36%)
  matrix products  53.5 us (26%)
  local copies, waits for them, and re-layouts  42 us (21%)
  waiting for transfers between devices  21.1 us (10%)
  other arithmetic  6.91 us (3%)
  starting transfers between devices  3.6 us (2%)
    psum x1, blocking collectives, per_device(): lax.psum((piece_up_weight, piece_down_weight, part_up_o, part_down_o), ('...  72.6 us
    ppermute x2, waiting for transfers between devices, passed_along(): return lax.ppermute(x, axis, [(i, (i + by) % peers) for i in range(peers)])  21.1 us
    unnamed x50, local copies, waits for them, and re-layouts  9.55 us
    dot_general x1, matrix products, per_device(): jnp.einsum('td,hd->th', cotangent, output_weight, preferred_element_type=...  9.48 us
    reshape x6, local copies, waits for them, and re-layouts, join_heads(): return tensor.reshape(tensor.shape[0], -1)  8.38 us
    sub x2, matrix products, attend(): raised = jnp.exp(scores - row_max)  8.17 us
    dot_general x2, matrix products, attend(): jnp.einsum('hqk,khe->qhe', probs_low, values, preferred_element_type=jnp....  6.46 us
    dynamic_slice x6, local copies, waits for them, and re-layouts, take_half(): return lax.dynamic_slice_in_dim(matrix, offset, half_width, axis_index)  6.39 us
  transfers between devices with their start and end apart: 2, of which 2 were waited for; matrix products, arithmetic and copies ran while one was open for 27% of the time, Pallas kernels for 0%

commit v1 on v0

v1 whole, which is shorter than its diff:
```python
import functools
import math

import jax
import jax.numpy as jnp
from jax import lax
from jax.experimental import pallas as pl
from jax.experimental.pallas import tpu as pltpu
from jax.sharding import PartitionSpec as P

MESH = pl.DeviceIdType.MESH
DMA = pltpu.SemaphoreType.DMA
VMEM = pltpu.VMEM
F32 = jnp.float32
BF16 = jnp.bfloat16

TOKENS = 256
MODEL = 4096
HEADS_WIDTH = 2048
HALF = 1024
HEAD = 128
RANK = 8
CTX = 32
SCALE = 1.0 / math.sqrt(HEAD)
EXP2_SCALE = SCALE * math.log2(math.e)
GRAD_SCALE = 2.0 / 32768
OW_BLOCK = 512

DOWN_AT = 0
UP_O_AT = 3 * MODEL
UP_AT = 4 * MODEL
DOWN_O_AT = 4 * MODEL + 3 * HEADS_WIDTH
PACKED = 4 * MODEL + 4 * HEADS_WIDTH
PACKED_HALF = PACKED // 2
CORE_LANES = PACKED // 4
PLANE = 16
CHUNK = CORE_LANES // PLANE


def nn(a, b):
    return lax.dot_general(a, b, (((1,), (0,)), ((), ())), preferred_element_type=F32)


def nt(a, b):
    return lax.dot_general(a, b, (((1,), (1,)), ((), ())), preferred_element_type=F32)


def tn(a, b):
    return lax.dot_general(a, b, (((0,), (0,)), ((), ())), preferred_element_type=F32)


def lanes(start, size):
    return pl.ds(pl.multiple_of(start, 128), size)


def attention_kernel(
    hidden_hbm,
    projected_hbm,
    gradient_hbm,
    weight_hbm,
    down_ref,
    up_ref,
    down_o_ref,
    up_o_ref,
    d_low_ref,
    packed_ref,
    hid,
    q,
    k,
    v,
    og,
    ow,
    far_k,
    far_v,
    d_attn,
    att,
    dq,
    dk,
    dv,
    dk_far,
    dv_far,
    low_own,
    low_far,
    d_low_send,
    d_low_recv,
    in_sem,
    ow_sem,
    qkv_sem,
    kv_send_sem,
    kv_recv_sem,
    small_send_sem,
    small_recv_sem,
):
    dp = lax.axis_index("dp")
    ctx = lax.axis_index("ctx")
    following = (dp, lax.rem(ctx + 1, CTX))
    previous = (dp, lax.rem(ctx + CTX - 1, CTX))
    parity = lax.rem(ctx, 2)
    first_start = parity * HALF
    pair_start = (1 - parity) * HALF

    barrier = pltpu.get_barrier_semaphore()
    pl.semaphore_signal(barrier, inc=1, device_id=following, device_id_type=MESH)
    pl.semaphore_signal(barrier, inc=1, device_id=previous, device_id_type=MESH)

    def ow_copy(block):
        half = block // (HALF // OW_BLOCK)
        start = jnp.where(half == 0, first_start, pair_start)
        row = start + lax.rem(block, HALF // OW_BLOCK) * OW_BLOCK
        return pltpu.make_async_copy(
            weight_hbm.at[pl.ds(pl.multiple_of(row, OW_BLOCK), OW_BLOCK), :],
            ow.at[pl.ds(pl.multiple_of(block * OW_BLOCK, OW_BLOCK), OW_BLOCK), :],
            ow_sem.at[block],
        )

    og_copy = pltpu.make_async_copy(gradient_hbm.at[0], og, in_sem.at[0])
    hid_copy = pltpu.make_async_copy(hidden_hbm.at[0], hid, in_sem.at[1])
    qkv_copies = [
        [
            pltpu.make_async_copy(
                projected_hbm.at[c, 0, :, lanes(start, HALF)],
                ref.at[:, at * HALF : (at + 1) * HALF],
                qkv_sem.at[at, c],
            )
            for c, ref in enumerate((q, k, v))
        ]
        for at, start in enumerate((first_start, pair_start))
    ]
    og_copy.start()
    hid_copy.start()
    ow_copy(0).start()
    ow_copy(1).start()
    for copy in qkv_copies[0]:
        copy.start()
    ow_copy(2).start()
    ow_copy(3).start()
    for copy in qkv_copies[1]:
        copy.start()

    pl.semaphore_wait(barrier, 2)
    kv_copies = []
    for j in range(4):
        for c, ref in ((0, far_k), (1, far_v)):
            copy = pltpu.make_async_remote_copy(
                src_ref=projected_hbm.at[c + 1, 0, :, lanes(first_start + j * 256, 256)],
                dst_ref=ref.at[:, j * 256 : (j + 1) * 256],
                send_sem=kv_send_sem.at[j, c],
                recv_sem=kv_recv_sem.at[j, c],
                device_id=following,
                device_id_type=MESH,
            )
            copy.start()
            kv_copies.append(copy)

    og_copy.wait()
    dy_low = nt(up_o_ref[...], og[...]).astype(BF16)
    hid_copy.wait()
    low_in = nt(down_ref[...], hid[...]).astype(BF16)
    low_own[...] = low_in[RANK:]
    low_copy = pltpu.make_async_remote_copy(
        src_ref=low_own,
        dst_ref=low_far,
        send_sem=small_send_sem.at[0],
        recv_sem=small_recv_sem.at[0],
        device_id=following,
        device_id_type=MESH,
    )
    low_copy.start()

    def project(block, carry):
        ow_copy(block).wait()
        half = block // (HALF // OW_BLOCK)
        start = jnp.where(half == 0, first_start, pair_start)
        column = start + lax.rem(block, HALF // OW_BLOCK) * OW_BLOCK
        rows = pl.ds(pl.multiple_of(block * OW_BLOCK, OW_BLOCK), OW_BLOCK)
        through_adapter = tn(down_o_ref[:, lanes(column, OW_BLOCK)], dy_low)
        d_attn[rows, :] = (nt(ow[rows, :], og[...]) + 2.0 * through_adapter).astype(BF16)
        return carry

    lax.fori_loop(0, HEADS_WIDTH // OW_BLOCK, project, 0)

    key_row = lax.broadcasted_iota(jnp.int32, (TOKENS, TOKENS), 0)
    query_column = lax.broadcasted_iota(jnp.int32, (TOKENS, TOKENS), 1)
    seen = key_row <= query_column

    def head(at, far_at):
        cols = lanes(at, HEAD)
        rows = pl.ds(pl.multiple_of(at, HEAD), HEAD)
        q_head = q[:, cols]
        d_head = d_attn[rows, :]
        keys = [k[:, cols]]
        values = [v[:, cols]]
        if far_at is not None:
            far_cols = lanes(far_at, HEAD)
            keys.append(far_k[:, far_cols])
            values.append(far_v[:, far_cols])
        scores = [nt(key, q_head) * EXP2_SCALE for key in keys]
        scores[0] = jnp.where(seen, scores[0], -jnp.inf)
        row_max = functools.reduce(
            jnp.maximum, [jnp.max(score, axis=0, keepdims=True) for score in scores]
        )
        raised = [jnp.exp2(score - row_max) for score in scores]
        total = sum(jnp.sum(r, axis=0, keepdims=True) for r in raised)
        inverse = 1.0 / total
        probs = [r * inverse for r in raised]
        probs_low = [p.astype(BF16) for p in probs]
        d_probs = [nn(value, d_head) for value in values]
        row_dot = sum(
            jnp.sum(p * d, axis=0, keepdims=True) for p, d in zip(probs, d_probs)
        )
        d_scores = [(p * (d - row_dot)).astype(BF16) for p, d in zip(probs, d_probs)]
        att[rows, :] = sum(tn(value, p) for value, p in zip(values, probs_low)).astype(BF16)
        dq[rows, :] = (sum(tn(key, s) for key, s in zip(keys, d_scores)) * SCALE).astype(BF16)
        dk[:, cols] = (nn(d_scores[0], q_head) * SCALE).astype(BF16)
        dv[:, cols] = nt(probs_low[0], d_head).astype(BF16)
        if far_at is not None:
            dk_far[:, far_cols] = (nn(d_scores[1], q_head) * SCALE).astype(BF16)
            dv_far[:, far_cols] = nt(probs_low[1], d_head).astype(BF16)

    for copy in qkv_copies[0]:
        copy.wait()

    def first_heads(j, carry):
        for i in range(2):
            head(j * 256 + i * HEAD, None)
        return carry

    lax.fori_loop(0, 4, first_heads, 0)
    for copy in qkv_copies[1]:
        copy.wait()

    def pair_heads(j, carry):
        for c, ref in ((0, far_k), (1, far_v)):
            part = ref.at[:, lanes(j * 256, 256)]
            pltpu.make_async_copy(part, part, kv_recv_sem.at[j, c]).wait()
        for i in range(2):
            head(HALF + j * 256 + i * HEAD, j * 256 + i * HEAD)
        return carry

    lax.fori_loop(0, 4, pair_heads, 0)

    halves = ((0, first_start), (HALF, pair_start))

    d_low_send[:RANK] = nt(up_ref[1, :, lanes(pair_start, HALF)], dk_far[...])
    d_low_send[RANK:] = nt(up_ref[2, :, lanes(pair_start, HALF)], dv_far[...])
    d_low_copy = pltpu.make_async_remote_copy(
        src_ref=d_low_send,
        dst_ref=d_low_recv,
        send_sem=small_send_sem.at[1],
        recv_sem=small_recv_sem.at[1],
        device_id=previous,
        device_id_type=MESH,
    )
    d_low_copy.start()

    low_o = sum(
        nn(down_o_ref[:, lanes(start, HALF)], att[at : at + HALF, :]) for at, start in halves
    ).astype(BF16)
    packed_ref[:, UP_O_AT : UP_O_AT + MODEL] = nn(low_o, og[...])
    for at, start in halves:
        packed_ref[:, lanes(DOWN_O_AT + start, HALF)] = nt(dy_low, att[at : at + HALF, :])
        packed_ref[:, lanes(UP_AT + start, HALF)] = nt(low_in[:RANK], dq[at : at + HALF, :])
    low_copy.wait()
    for c, near, far in ((1, dk, dk_far), (2, dv, dv_far)):
        own = low_in[c * RANK : (c + 1) * RANK]
        at_c = UP_AT + c * HEADS_WIDTH
        packed_ref[:, lanes(at_c + first_start, HALF)] = nn(own, near[:, :HALF])
        packed_ref[:, lanes(at_c + pair_start, HALF)] = nn(own, near[:, HALF:]) + nn(
            low_far[(c - 1) * RANK : c * RANK], far[...]
        )
    d_low = [
        sum(nn(up_ref[0, :, lanes(start, HALF)], dq[at : at + HALF, :]) for at, start in halves)
    ]
    for c, near in ((1, dk), (2, dv)):
        d_low.append(
            sum(
                nt(up_ref[c, :, lanes(start, HALF)], near[:, at : at + HALF])
                for at, start in halves
            )
        )
    d_low_copy.wait()
    d_low[1] += d_low_recv[:RANK]
    d_low[2] += d_low_recv[RANK:]
    d_low = jnp.concatenate(d_low, axis=0).astype(BF16)
    d_low_ref[...] = d_low
    down = nn(d_low, hid[...])
    for c in range(3):
        packed_ref[:, DOWN_AT + c * MODEL : DOWN_AT + (c + 1) * MODEL] = down[
            c * RANK : (c + 1) * RANK
        ]
    for copy in kv_copies:
        copy.wait_send()


def attention_part(hidden, projected, gradient, weight, down, up, down_o, up_o):
    half = VMEM((TOKENS, HALF), BF16)
    whole = VMEM((TOKENS, HEADS_WIDTH), BF16)
    flipped = VMEM((HEADS_WIDTH, TOKENS), BF16)
    wide = VMEM((TOKENS, MODEL), BF16)
    anywhere = pl.BlockSpec(memory_space=pl.ANY)
    resident = pl.BlockSpec(memory_space=VMEM)
    return pl.pallas_call(
        attention_kernel,
        out_shape=(
            jax.ShapeDtypeStruct((3 * RANK, TOKENS), BF16),
            jax.ShapeDtypeStruct((RANK, PACKED), F32),
        ),
        in_specs=[anywhere] * 4 + [resident] * 4,
        out_specs=(resident, resident),
        scratch_shapes=[
            wide,
            whole,
            whole,
            whole,
            wide,
            VMEM((HEADS_WIDTH, MODEL), BF16),
            half,
            half,
            flipped,
            flipped,
            flipped,
            whole,
            whole,
            half,
            half,
            VMEM((2 * RANK, TOKENS), BF16),
            VMEM((2 * RANK, TOKENS), BF16),
            VMEM((2 * RANK, TOKENS), F32),
            VMEM((2 * RANK, TOKENS), F32),
            DMA((2,)),
            DMA((4,)),
            DMA((2, 3)),
            DMA((4, 2)),
            DMA((4, 2)),
            DMA((2,)),
            DMA((2,)),
        ],
        compiler_params=pltpu.CompilerParams(
            collective_id=0, has_side_effects=True, vmem_limit_bytes=56 << 20
        ),
    )(hidden, projected, gradient, weight, down, up, down_o, up_o)


def reduce_kernel(
    part_ref,
    out_ref,
    pair_recv,
    low,
    plane_recv,
    mine,
    line_recv,
    pair_sems,
    plane_send,
    plane_recv_sem,
    line_send,
    line_recv_sem,
    back_send,
    back_recv_sem,
    last_sems,
):
    dp = lax.axis_index("dp")
    ctx = lax.axis_index("ctx")
    core = lax.rem(dp, 2)
    y_lo = dp // 2
    y_hi = ctx // PLANE
    place = lax.rem(ctx, PLANE)
    y = y_hi * 2 + y_lo

    def plane_peer(r):
        return (dp, y_hi * PLANE + lax.rem(place + r, PLANE))

    def line_peer(r):
        other_y = lax.rem(y + r, 4)
        return (lax.rem(other_y, 2) * 2 + core, (other_y // 2) * PLANE + place)

    other_core = (y_lo * 2 + 1 - core, ctx)
    barrier = pltpu.get_barrier_semaphore()
    pl.semaphore_signal(barrier, inc=1, device_id=other_core, device_id_type=MESH)
    for r in range(1, PLANE):
        pl.semaphore_signal(barrier, inc=1, device_id=plane_peer(r), device_id_type=MESH)
    for r in range(1, 4):
        pl.semaphore_signal(barrier, inc=1, device_id=line_peer(r), device_id_type=MESH)
    pl.semaphore_wait(barrier, PLANE + 3)

    pair_copies = []
    for row in range(2):
        copy = pltpu.make_async_remote_copy(
            src_ref=part_ref.at[
                :, lanes(row * PACKED_HALF + (1 - core) * CORE_LANES, CORE_LANES)
            ],
            dst_ref=pair_recv.at[row],
            send_sem=pair_sems.at[row, 0],
            recv_sem=pair_sems.at[row, 1],
            device_id=other_core,
            device_id_type=MESH,
        )
        copy.start()
        pair_copies.append(copy)
    for copy in pair_copies:
        copy.wait()
    for n in range(PLANE):
        rows = [
            part_ref[:, lanes(row * PACKED_HALF + core * CORE_LANES + n * CHUNK, CHUNK)]
            + pair_recv[row, :, n * CHUNK : (n + 1) * CHUNK]
            for row in range(2)
        ]
        low[n] = jnp.concatenate(rows, axis=0).astype(BF16)

    for r in range(1, PLANE):
        pltpu.make_async_remote_copy(
            src_ref=low.at[lax.rem(place + r, PLANE)],
            dst_ref=plane_recv.at[r - 1],
            send_sem=plane_send,
            recv_sem=plane_recv_sem,
            device_id=plane_peer(r),
            device_id_type=MESH,
        ).start()
    total = low[place].astype(F32)
    pltpu.make_async_copy(plane_recv, plane_recv, plane_recv_sem).wait()
    for r in range(PLANE - 1):
        total = total + plane_recv[r].astype(F32)
    mine[...] = total.astype(BF16)
    line_recv[y] = mine[...]
    for r in range(1, 4):
        pltpu.make_async_remote_copy(
            src_ref=mine,
            dst_ref=line_recv.at[y],
            send_sem=line_send,
            recv_sem=line_recv_sem,
            device_id=line_peer(r),
            device_id_type=MESH,
        ).start()
    three = line_recv.at[0:3]
    pltpu.make_async_copy(three, three, line_recv_sem).wait()
    total = line_recv[0].astype(F32)
    for r in range(1, 4):
        total = total + line_recv[r].astype(F32)
    out_ref[core, place] = (total * GRAD_SCALE).astype(BF16)
    for r in range(1, PLANE):
        pltpu.make_async_remote_copy(
            src_ref=out_ref.at[core, place],
            dst_ref=out_ref.at[core, place],
            send_sem=back_send,
            recv_sem=back_recv_sem,
            device_id=plane_peer(r),
            device_id_type=MESH,
        ).start()
    pltpu.make_async_copy(plane_recv, plane_recv, back_recv_sem).wait()
    last = pltpu.make_async_remote_copy(
        src_ref=out_ref.at[core],
        dst_ref=out_ref.at[core],
        send_sem=last_sems.at[0],
        recv_sem=last_sems.at[1],
        device_id=other_core,
        device_id_type=MESH,
    )
    last.start()
    pltpu.make_async_copy(plane_recv, plane_recv, plane_send).wait()
    pltpu.make_async_copy(three, three, line_send).wait()
    pltpu.make_async_copy(plane_recv, plane_recv, back_send).wait()
    last.wait()


def reduce_part(packed):
    resident = pl.BlockSpec(memory_space=VMEM)
    return pl.pallas_call(
        reduce_kernel,
        out_shape=jax.ShapeDtypeStruct((2, PLANE, 16, CHUNK), BF16),
        in_specs=[resident],
        out_specs=resident,
        scratch_shapes=[
            VMEM((2, RANK, CORE_LANES), F32),
            VMEM((PLANE, 16, CHUNK), BF16),
            VMEM((PLANE - 1, 16, CHUNK), BF16),
            VMEM((16, CHUNK), BF16),
            VMEM((4, 16, CHUNK), BF16),
            DMA((2, 2)),
            DMA,
            DMA,
            DMA,
            DMA,
            DMA,
            DMA,
            DMA((2,)),
        ],
        compiler_params=pltpu.CompilerParams(
            collective_id=1, has_side_effects=True, vmem_limit_bytes=32 << 20
        ),
    )(packed)


def finish_kernel(
    summed_ref, d_low_ref, down_ref, input_ref, grad_down_ref, grad_up_ref, down_o_ref, up_o_ref
):
    def place(tile, value):
        at = tile * 128
        if at < UP_O_AT:
            c, at = divmod(at, MODEL)
            grad_down_ref[c, :, at : at + 128] = value
        elif at < UP_AT:
            at -= UP_O_AT
            up_o_ref[:, at : at + 128] = value
        elif at < DOWN_O_AT:
            c, at = divmod(at - UP_AT, HEADS_WIDTH)
            grad_up_ref[c, :, at : at + 128] = value
        else:
            at -= DOWN_O_AT
            down_o_ref[:, at : at + 128] = value

    for core in range(2):
        for n in range(PLANE):
            for t in range(CHUNK // 128):
                block = summed_ref[core, n, :, t * 128 : (t + 1) * 128].astype(F32)
                tile = (core * CORE_LANES + n * CHUNK) // 128 + t
                for row in range(2):
                    place(
                        row * PACKED_HALF // 128 + tile,
                        block[row * RANK : (row + 1) * RANK].astype(BF16),
                    )
    for n in range(MODEL // 512):
        cols = slice(n * 512, (n + 1) * 512)
        input_ref[0, :, cols] = (2.0 * tn(d_low_ref[...], down_ref[:, cols])).astype(BF16)


def finish_part(summed, d_low, down):
    resident = pl.BlockSpec(memory_space=VMEM)
    return pl.pallas_call(
        finish_kernel,
        out_shape=(
            jax.ShapeDtypeStruct((1, TOKENS, MODEL), BF16),
            jax.ShapeDtypeStruct((3, RANK, MODEL), BF16),
            jax.ShapeDtypeStruct((3, RANK, HEADS_WIDTH), BF16),
            jax.ShapeDtypeStruct((RANK, HEADS_WIDTH), BF16),
            jax.ShapeDtypeStruct((RANK, MODEL), BF16),
        ),
        in_specs=[resident] * 3,
        out_specs=(resident,) * 5,
        compiler_params=pltpu.CompilerParams(vmem_limit_bytes=32 << 20),
    )(summed, d_low, down)


def per_device(hidden, projected, gradient, weight, down, up, down_o, up_o):
    down = down.reshape(3 * RANK, MODEL)
    d_low, packed = attention_part(hidden, projected, gradient, weight, down, up, down_o, up_o)
    summed = reduce_part(packed)
    return finish_part(summed, d_low, down)


def solution(mesh):
    in_specs = (
        P("dp", "ctx", None),
        P(None, "dp", "ctx", None),
        P("dp", "ctx", None),
        P(),
        P(),
        P(),
        P(),
        P(),
    )
    out_specs = (P("dp", "ctx", None), P(), P(), P(), P())
    return jax.shard_map(
        per_device, mesh=mesh, in_specs=in_specs, out_specs=out_specs, check_vma=False
    )
```

time: 202 us -> 69.2 us (0.34)
  blocking collectives: 72.6 us -> 0 us
  Pallas kernels: 0 us -> 66.5 us
  matrix products: 53.5 us -> 0 us
  local copies, waits for them, and re-layouts: 42 us -> 1.83 us
  waiting for transfers between devices: 21.1 us -> 0 us
  other arithmetic: 6.91 us -> 0 us
  starting transfers between devices: 3.6 us -> 0 us
    psum x1 -> x0, blocking collectives: 72.6 us -> none  [per_device(): lax.psum((piece_up_weight, piece_down_weight, part_up_o, part_down_o), ('...]
    pallas_call x0 -> x3, Pallas kernels: none -> 66.5 us  [the longest x1 39.6 us: attention_part(): pl.pallas_call(attention_kernel, out_shape=(jax.ShapeDtypeStruct((3 * RAN...]
    dot_general x19 -> x0, matrix products: 45.4 us -> none  [the longest x1 9.48 us: per_device(): jnp.einsum('td,hd->th', cotangent, output_weight, preferred_element_type=...]
    ppermute x2 -> x0, waiting for transfers between devices: 21.1 us -> none  [passed_along(): return lax.ppermute(x, axis, [(i, (i + by) % peers) for i in range(peers)])]
    slice x6 -> x0, local copies, waits for them, and re-layouts: 9.09 us -> none  [the longest x1 3.31 us: per_device(): key_value = projected[1:, 0]]
    reshape x6 -> x0, local copies, waits for them, and re-layouts: 8.38 us -> none  [join_heads(): return tensor.reshape(tensor.shape[0], -1)]
    sub x2 -> x0, matrix products: 8.17 us -> none  [attend(): raised = jnp.exp(scores - row_max)]
    unnamed x50 -> x6, local copies, waits for them, and re-layouts: 9.55 us -> 1.83 us
  transfers between devices with their start and end apart: 2 -> 0, of which waited for: 2 -> 0; matrix products, arithmetic and copies ran while one was open for 27% -> 0% of each run, Pallas kernels for 0% -> 0%
where the time goes in v1:
time: 69.2 us; the launch traced here: 69 us
  Pallas kernels  66.5 us (96%)
  local copies, waits for them, and re-layouts  1.83 us (3%)
    pallas_call x1, Pallas kernels, attention_part(): pl.pallas_call(attention_kernel, out_shape=(jax.ShapeDtypeStruct((3 * RAN...  39.6 us
    pallas_call x1, Pallas kernels, reduce_part(): pl.pallas_call(reduce_kernel, out_shape=jax.ShapeDtypeStruct((2, PLANE, 1...  24.8 us
    pallas_call x1, Pallas kernels, finish_part(): pl.pallas_call(finish_kernel, out_shape=(jax.ShapeDtypeStruct((1, TOKENS,...  2.17 us
    unnamed x6, local copies, waits for them, and re-layouts  1.83 us

profile of v1, /device:TPU:1, one launch (start us, length us, event | category | flops | bytes accessed | tf_op | source)
XLA Modules:
  0.0 69.0 jit_solution(6867682918244110386)
XLA Ops:
  0.6 0.0 copy-start
  0.6 39.6 %shard_map.119 = (bf16[24,256]{1,0:T(8,128)(2,1)}, f32[8,24576]{1,0:T(8,128)}) custom-call(bf16[1,256,4096]{2,1,0:T(8,128)(2,1)} %hidden_hbm.1, bf16[3,1,256,2048]{3,2,1,0:T(8,128)(2,1)} %projected_hbm.1, bf16[1,256,4096]{2,1,0:T(8,128)(2,1)} %gradient_hbm.1, bf16[2048,4096]{1,0:T(8,128)(2,1)} %weight_hbm.1, bf16[24,4096]{1,0:T(8,128)(2,1)} %bitcast.1, ...), custom_call_target="tpu_custom_call" | custom-call | tf_op jit(solution)/shard_map/pallas_call | solution.py:302
  40.2 0.0 copy-start.1
  40.2 1.1 %copy-done.1 = f32[8,24576]{1,0:T(8,128)S(1)} copy-done((f32[8,24576]{1,0:T(8,128)S(1)}, f32[8,24576]{1,0:T(8,128)}, u32[]{:S(2)}) %copy-start.1) | copy-done | bytes 786456
  41.3 24.8 %shard_map.120.summed_ref = bf16[2,16,16,384]{3,2,1,0:T(8,128)(2,1)S(1)} custom-call(f32[8,24576]{1,0:T(8,128)S(1)} %copy-done.1), custom_call_target="tpu_custom_call" | custom-call | tf_op jit(solution)/shard_map/pallas_call | solution.py:466
  66.1 0.0 copy-done
  66.1 0.0 copy-start.2
  66.1 0.7 %copy-done.2 = bf16[24,256]{1,0:T(8,128)(2,1)S(1)} copy-done((bf16[24,256]{1,0:T(8,128)(2,1)S(1)}, bf16[24,256]{1,0:T(8,128)(2,1)}, u32[]{:S(2)}) %copy-start.2) | copy-done | bytes 12312
  66.8 2.2 %shard_map.121 = (bf16[1,256,4096]{2,1,0:T(8,128)(2,1)}, bf16[3,8,4096]{2,1,0:T(8,128)(2,1)}, bf16[3,8,2048]{2,1,0:T(8,128)(2,1)}, bf16[8,2048]{1,0:T(8,128)(2,1)}, bf16[8,4096]{1,0:T(8,128)(2,1)}) custom-call(bf16[2,16,16,384]{3,2,1,0:T(8,128)(2,1)S(1)} %shard_map.120.summed_ref, bf16[24,256]{1,0:T(8,128)(2,1)S(1)} %copy-done.2, bf16[24,4096]{1,0:T(8,128)(2,1)S(1)} %bitcast.2), custom_call_target="tpu_custom_call" | custom-call | tf_op jit(solution)/shard_map/pallas_call | solution.py:527
Async XLA Ops:
  0.6 65.5 %copy-start = (bf16[3,8,4096]{2,1,0:T(8,128)(2,1)S(1)}, bf16[3,8,4096]{2,1,0:T(8,128)(2,1)}, u32[]{:S(2)}) copy-start(bf16[3,8,4096]{2,1,0:T(8,128)(2,1)} %param.12) | copy-start | bytes 589828
  40.2 1.1 %copy-start.1 = (f32[8,24576]{1,0:T(8,128)S(1)}, f32[8,24576]{1,0:T(8,128)}, u32[]{:S(2)}) copy-start(f32[8,24576]{1,0:T(8,128)} %get-tuple-element.7.part_ref) | copy-start | bytes 2359300
  66.1 0.7 %copy-start.2 = (bf16[24,256]{1,0:T(8,128)(2,1)S(1)}, bf16[24,256]{1,0:T(8,128)(2,1)}, u32[]{:S(2)}) copy-start(bf16[24,256]{1,0:T(8,128)(2,1)} %get-tuple-element.8.d_low_ref) | copy-start | bytes 36868

commit v2 on v1

v2 whole, which is shorter than its diff:
```python
import functools
import math

import jax
import jax.numpy as jnp
from jax import lax
from jax.experimental import pallas as pl
from jax.experimental.pallas import tpu as pltpu
from jax.sharding import PartitionSpec as P

MESH = pl.DeviceIdType.MESH
DMA = pltpu.SemaphoreType.DMA
VMEM = pltpu.VMEM
F32 = jnp.float32
BF16 = jnp.bfloat16

TOKENS = 256
MODEL = 4096
HEADS_WIDTH = 2048
HALF = 1024
HEAD = 128
RANK = 8
CTX = 32
SCALE = 1.0 / math.sqrt(HEAD)
EXP2_SCALE = SCALE * math.log2(math.e)
GRAD_SCALE = 2.0 / 32768
OW_BLOCK = 512

TILE = 128
LATE_SLOTS = 32
SLOTS = 48
DEVICES = 128


def nn(a, b):
    return lax.dot_general(a, b, (((1,), (0,)), ((), ())), preferred_element_type=F32)


def nt(a, b):
    return lax.dot_general(a, b, (((1,), (1,)), ((), ())), preferred_element_type=F32)


def tn(a, b):
    return lax.dot_general(a, b, (((0,), (0,)), ((), ())), preferred_element_type=F32)


def lanes(start, size):
    return pl.ds(pl.multiple_of(start, 128), size)


def stacked(top, bottom):
    return jnp.concatenate([top, bottom], axis=0).astype(BF16)


def tile_of(value, n):
    return value[:, n * TILE : (n + 1) * TILE]


def away(ctx, j, wide):
    x = lax.rem(ctx // 4 % 4 + 2 + j // 4 % 4, 4)
    z = lax.rem(ctx % 4 + 2 + j % 4, 4)
    if not wide:
        return x * 4 + z
    return lax.rem(ctx // 16 + 1 + j // 16 % 2, 2) * 16 + x * 4 + z


def attention_kernel(
    hidden_hbm,
    projected_hbm,
    gradient_hbm,
    weight_hbm,
    down_ref,
    up_ref,
    down_o_ref,
    up_o_ref,
    d_low_ref,
    summed_ref,
    hid,
    q,
    k,
    v,
    og,
    ow,
    far_k,
    far_v,
    d_attn,
    att,
    dq,
    dk,
    dv,
    dk_far,
    dv_far,
    low_own,
    low_far,
    d_low_send,
    d_low_recv,
    low,
    parts,
    in_sem,
    ow_sem,
    qkv_sem,
    kv_send_sem,
    kv_recv_sem,
    small_send_sem,
    small_recv_sem,
    part_send_sem,
    part_recv_sem,
    sum_send_sem,
    sum_recv_sem,
    last_sems,
):
    dp = lax.axis_index("dp")
    ctx = lax.axis_index("ctx")
    following = (dp, lax.rem(ctx + 1, CTX))
    previous = (dp, lax.rem(ctx + CTX - 1, CTX))
    parity = lax.rem(ctx, 2)
    first_start = parity * HALF
    pair_start = (1 - parity) * HALF

    core = lax.rem(dp, 2)
    y_lo = dp // 2
    me = dp * CTX + ctx

    barrier = pltpu.get_barrier_semaphore()

    def greet(n, carry):
        other = lax.rem(me + n, DEVICES)
        pl.semaphore_signal(
            barrier, inc=1, device_id=(other // CTX, lax.rem(other, CTX)), device_id_type=MESH
        )
        return carry

    def ow_copy(block):
        half = block // (HALF // OW_BLOCK)
        start = jnp.where(half == 0, first_start, pair_start)
        row = start + lax.rem(block, HALF // OW_BLOCK) * OW_BLOCK
        return pltpu.make_async_copy(
            weight_hbm.at[pl.ds(pl.multiple_of(row, OW_BLOCK), OW_BLOCK), :],
            ow.at[pl.ds(pl.multiple_of(block * OW_BLOCK, OW_BLOCK), OW_BLOCK), :],
            ow_sem.at[block],
        )

    og_copy = pltpu.make_async_copy(gradient_hbm.at[0], og, in_sem.at[0])
    hid_copy = pltpu.make_async_copy(hidden_hbm.at[0], hid, in_sem.at[1])
    qkv_copies = [
        [
            pltpu.make_async_copy(
                projected_hbm.at[c, 0, :, lanes(start, HALF)],
                ref.at[:, at * HALF : (at + 1) * HALF],
                qkv_sem.at[at, c],
            )
            for c, ref in enumerate((q, k, v))
        ]
        for at, start in enumerate((first_start, pair_start))
    ]
    og_copy.start()
    ow_copy(0).start()
    lax.fori_loop(1, DEVICES, greet, 0)
    pl.semaphore_wait(barrier, DEVICES - 1)
    kv_copies = []
    for j in range(4):
        for c, ref in ((0, far_k), (1, far_v)):
            copy = pltpu.make_async_remote_copy(
                src_ref=projected_hbm.at[c + 1, 0, :, lanes(first_start + j * 256, 256)],
                dst_ref=ref.at[:, j * 256 : (j + 1) * 256],
                send_sem=kv_send_sem.at[j, c],
                recv_sem=kv_recv_sem.at[j, c],
                device_id=following,
                device_id_type=MESH,
            )
            copy.start()
            kv_copies.append(copy)

    ow_copy(1).start()
    hid_copy.start()
    og_copy.wait()
    dy_low = nt(up_o_ref[...], og[...]).astype(BF16)

    def project(block, carry):
        ow_copy(block).wait()

        @pl.when(block < 2)
        def _():
            ow_copy(block + 2).start()

        half = block // (HALF // OW_BLOCK)
        start = jnp.where(half == 0, first_start, pair_start)
        column = start + lax.rem(block, HALF // OW_BLOCK) * OW_BLOCK
        rows = pl.ds(pl.multiple_of(block * OW_BLOCK, OW_BLOCK), OW_BLOCK)
        through_adapter = tn(down_o_ref[:, lanes(column, OW_BLOCK)], dy_low)
        d_attn[rows, :] = (nt(ow[rows, :], og[...]) + 2.0 * through_adapter).astype(BF16)
        return carry

    lax.fori_loop(0, 2, project, 0)
    for copies in qkv_copies:
        for copy in copies:
            copy.start()
    hid_copy.wait()
    low_in = nt(down_ref[...], hid[...]).astype(BF16)
    low_own[...] = low_in[RANK:]
    low_copy = pltpu.make_async_remote_copy(
        src_ref=low_own,
        dst_ref=low_far,
        send_sem=small_send_sem.at[0],
        recv_sem=small_recv_sem.at[0],
        device_id=following,
        device_id_type=MESH,
    )
    low_copy.start()
    lax.fori_loop(2, 4, project, 0)

    key_row = lax.broadcasted_iota(jnp.int32, (TOKENS, TOKENS), 0)
    query_column = lax.broadcasted_iota(jnp.int32, (TOKENS, TOKENS), 1)
    seen = key_row <= query_column

    def head(at, far_at):
        cols = lanes(at, HEAD)
        rows = pl.ds(pl.multiple_of(at, HEAD), HEAD)
        q_head = q[:, cols]
        d_head = d_attn[rows, :]
        keys = [k[:, cols]]
        values = [v[:, cols]]
        if far_at is not None:
            far_cols = lanes(far_at, HEAD)
            keys.append(far_k[:, far_cols])
            values.append(far_v[:, far_cols])
        scores = [nt(key, q_head) * EXP2_SCALE for key in keys]
        scores[0] = jnp.where(seen, scores[0], -jnp.inf)
        row_max = functools.reduce(
            jnp.maximum, [jnp.max(score, axis=0, keepdims=True) for score in scores]
        )
        raised = [jnp.exp2(score - row_max) for score in scores]
        total = sum(jnp.sum(r, axis=0, keepdims=True) for r in raised)
        inverse = 1.0 / total
        probs = [r * inverse for r in raised]
        probs_low = [p.astype(BF16) for p in probs]
        d_probs = [nn(value, d_head) for value in values]
        row_dot = sum(
            jnp.sum(p * d, axis=0, keepdims=True) for p, d in zip(probs, d_probs)
        )
        d_scores = [(p * (d - row_dot)).astype(BF16) for p, d in zip(probs, d_probs)]
        att[rows, :] = sum(tn(value, p) for value, p in zip(values, probs_low)).astype(BF16)
        dq[rows, :] = (sum(tn(key, s) for key, s in zip(keys, d_scores)) * SCALE).astype(BF16)
        dk[:, cols] = (nn(d_scores[0], q_head) * SCALE).astype(BF16)
        dv[:, cols] = nt(probs_low[0], d_head).astype(BF16)
        if far_at is not None:
            dk_far[:, far_cols] = (nn(d_scores[1], q_head) * SCALE).astype(BF16)
            dv_far[:, far_cols] = nt(probs_low[1], d_head).astype(BF16)

    for copy in qkv_copies[0]:
        copy.wait()

    def first_heads(j, carry):
        for i in range(2):
            head(j * 256 + i * HEAD, None)
        return carry

    lax.fori_loop(0, 4, first_heads, 0)
    for copy in qkv_copies[1]:
        copy.wait()

    def pair_heads(j, carry):
        for c, ref in ((0, far_k), (1, far_v)):
            part = ref.at[:, lanes(j * 256, 256)]
            pltpu.make_async_copy(part, part, kv_recv_sem.at[j, c]).wait()
        for i in range(2):
            head(HALF + j * 256 + i * HEAD, j * 256 + i * HEAD)
        return carry

    lax.fori_loop(0, 4, pair_heads, 0)

    halves = ((0, first_start), (HALF, pair_start))

    d_low_send[:RANK] = nt(up_ref[1, :, lanes(pair_start, HALF)], dk_far[...])
    d_low_send[RANK:] = nt(up_ref[2, :, lanes(pair_start, HALF)], dv_far[...])
    d_low_copy = pltpu.make_async_remote_copy(
        src_ref=d_low_send,
        dst_ref=d_low_recv,
        send_sem=small_send_sem.at[1],
        recv_sem=small_recv_sem.at[1],
        device_id=previous,
        device_id_type=MESH,
    )
    d_low_copy.start()

    def send_tiles(kind, base, count, late):
        def send(j, carry):
            to = away(ctx, j, count == 32) + (base % 32)
            to_y = lax.rem(to + kind + (0 if late else 1), 2)
            to_dp = to_y * 2 + kind
            slot = to + (0 if late else LATE_SLOTS)

            @pl.when(jnp.logical_or(to != ctx, to_dp != dp))
            def _():
                pltpu.make_async_remote_copy(
                    src_ref=low.at[kind * SLOTS + slot],
                    dst_ref=parts.at[me],
                    send_sem=part_send_sem,
                    recv_sem=part_recv_sem,
                    device_id=(to_dp, to),
                    device_id_type=MESH,
                ).start()

            return carry

        lax.fori_loop(0, count, send, 0)

    low_o = sum(
        nn(down_o_ref[:, lanes(start, HALF)], att[at : at + HALF, :]) for at, start in halves
    ).astype(BF16)
    up_o = nn(low_o, og[...])
    for n in range(16):
        low[SLOTS + 16 + n] = stacked(tile_of(up_o, n), tile_of(up_o, n + 16))
    send_tiles(1, 16, 16, True)

    low_copy.wait()
    for at, start in halves:
        up = [
            nt(low_in[:RANK], dq[at : at + HALF, :]),
            nn(low_in[RANK : 2 * RANK], dk[:, at : at + HALF]),
            nn(low_in[2 * RANK :], dv[:, at : at + HALF]),
        ]
        if at:
            up[1] += nn(low_far[:RANK], dk_far[...])
            up[2] += nn(low_far[RANK:], dv_far[...])
        down_o = nt(dy_low, att[at : at + HALF, :])
        slot = LATE_SLOTS + start // TILE
        for n in range(HALF // TILE):
            low[slot + n] = stacked(tile_of(up[0], n), tile_of(up[1], n))
            low[SLOTS + slot + n] = stacked(tile_of(up[2], n), tile_of(down_o, n))
    send_tiles(0, 0, 16, False)
    send_tiles(1, 0, 16, False)

    d_low = [
        sum(nn(up_ref[0, :, lanes(start, HALF)], dq[at : at + HALF, :]) for at, start in halves)
    ]
    for c, near in ((1, dk), (2, dv)):
        d_low.append(
            sum(
                nt(up_ref[c, :, lanes(start, HALF)], near[:, at : at + HALF])
                for at, start in halves
            )
        )
    d_low_copy.wait()
    d_low[1] += d_low_recv[:RANK]
    d_low[2] += d_low_recv[RANK:]
    d_low = jnp.concatenate(d_low, axis=0).astype(BF16)
    d_low_ref[...] = d_low
    down = nn(d_low, hid[...])
    third = down[2 * RANK :]
    for n in range(32):
        low[n] = tile_of(down[: 2 * RANK], n).astype(BF16)
    for n in range(16):
        low[SLOTS + n] = stacked(tile_of(third, n), tile_of(third, n + 16))
    send_tiles(0, 0, 32, True)
    send_tiles(1, 0, 16, True)

    is_late = lax.rem(ctx + core, 2) == y_lo
    is_owner = jnp.logical_or(is_late, ctx < 16)
    slot = jnp.where(is_late, ctx, LATE_SLOTS + ctx)

    @pl.when(is_owner)
    def _():
        parts[me] = low[core * SLOTS + slot]
        arriving = parts.at[0 : DEVICES - 1]
        pltpu.make_async_copy(arriving, arriving, part_recv_sem).wait()

        def add(n, total):
            return total + parts[n].astype(F32)

        total = lax.fori_loop(0, DEVICES, add, jnp.zeros((16, TILE), F32), unroll=8)
        summed_ref[core, slot] = (total * GRAD_SCALE).astype(BF16)

        def spread(j, carry):
            to = away(ctx, j, True)
            to_y = lax.rem(y_lo + 1 + j // 32, 2)

            @pl.when(jnp.logical_or(to != ctx, to_y != y_lo))
            def _():
                pltpu.make_async_remote_copy(
                    src_ref=summed_ref.at[core, slot],
                    dst_ref=summed_ref.at[core, slot],
                    send_sem=sum_send_sem,
                    recv_sem=sum_recv_sem,
                    device_id=(to_y * 2 + core, to),
                    device_id_type=MESH,
                ).start()

            return carry

        lax.fori_loop(0, 64, spread, 0)
        arriving = parts.at[0 : SLOTS - 1]
        pltpu.make_async_copy(arriving, arriving, sum_recv_sem).wait()

    @pl.when(jnp.logical_not(is_owner))
    def _():
        arriving = parts.at[0:SLOTS]
        pltpu.make_async_copy(arriving, arriving, sum_recv_sem).wait()

    last = pltpu.make_async_remote_copy(
        src_ref=summed_ref.at[core],
        dst_ref=summed_ref.at[core],
        send_sem=last_sems.at[0],
        recv_sem=last_sems.at[1],
        device_id=(y_lo * 2 + 1 - core, ctx),
        device_id_type=MESH,
    )
    last.start()

    @pl.when(is_owner)
    def _():
        sent = low.at[0 : 2 * SLOTS - 1]
        pltpu.make_async_copy(sent, sent, part_send_sem).wait()
        sent = low.at[0:63]
        pltpu.make_async_copy(sent, sent, sum_send_sem).wait()

    @pl.when(jnp.logical_not(is_owner))
    def _():
        pltpu.make_async_copy(low, low, part_send_sem).wait()

    for copy in kv_copies:
        copy.wait_send()
    last.wait()


def attention_part(hidden, projected, gradient, weight, down, up, down_o, up_o):
    half = VMEM((TOKENS, HALF), BF16)
    whole = VMEM((TOKENS, HEADS_WIDTH), BF16)
    flipped = VMEM((HEADS_WIDTH, TOKENS), BF16)
    wide = VMEM((TOKENS, MODEL), BF16)
    anywhere = pl.BlockSpec(memory_space=pl.ANY)
    resident = pl.BlockSpec(memory_space=VMEM)
    return pl.pallas_call(
        attention_kernel,
        out_shape=(
            jax.ShapeDtypeStruct((3 * RANK, TOKENS), BF16),
            jax.ShapeDtypeStruct((2, SLOTS, 16, TILE), BF16),
        ),
        in_specs=[anywhere] * 4 + [resident] * 4,
        out_specs=(resident, resident),
        scratch_shapes=[
            wide,
            whole,
            whole,
            whole,
            wide,
            VMEM((HEADS_WIDTH, MODEL), BF16),
            half,
            half,
            flipped,
            flipped,
            flipped,
            whole,
            whole,
            half,
            half,
            VMEM((2 * RANK, TOKENS), BF16),
            VMEM((2 * RANK, TOKENS), BF16),
            VMEM((2 * RANK, TOKENS), F32),
            VMEM((2 * RANK, TOKENS), F32),
            VMEM((2 * SLOTS, 16, TILE), BF16),
            VMEM((DEVICES, 16, TILE), BF16),
            DMA((2,)),
            DMA((4,)),
            DMA((2, 3)),
            DMA((4, 2)),
            DMA((4, 2)),
            DMA((2,)),
            DMA((2,)),
            DMA,
            DMA,
            DMA,
            DMA,
            DMA((2,)),
        ],
        compiler_params=pltpu.CompilerParams(
            collective_id=0, has_side_effects=True, vmem_limit_bytes=56 << 20
        ),
    )(hidden, projected, gradient, weight, down, up, down_o, up_o)


def finish_kernel(
    summed_ref,
    d_low_ref,
    down_ref,
    input_hbm,
    grad_down_ref,
    grad_up_ref,
    down_o_ref,
    up_o_ref,
    result,
    sems,
):
    copies = []
    for n in range(4):
        cols = slice(n * HALF, (n + 1) * HALF)
        result[:, cols] = (2.0 * tn(d_low_ref[...], down_ref[:, cols])).astype(BF16)
        copy = pltpu.make_async_copy(result.at[:, cols], input_hbm.at[0, :, cols], sems.at[n])
        copy.start()
        copies.append(copy)

    def halves_of(kind, slot):
        tile = summed_ref[kind, slot].astype(F32)
        return tile[:RANK].astype(BF16), tile[RANK:].astype(BF16)

    for n in range(32):
        cols = slice(n * TILE, (n + 1) * TILE)
        grad_down_ref[0, :, cols], grad_down_ref[1, :, cols] = halves_of(0, n)
    for n in range(16):
        cols = slice(n * TILE, (n + 1) * TILE)
        later = slice(HEADS_WIDTH + n * TILE, HEADS_WIDTH + (n + 1) * TILE)
        grad_down_ref[2, :, cols], grad_down_ref[2, :, later] = halves_of(1, n)
        up_o_ref[:, cols], up_o_ref[:, later] = halves_of(1, 16 + n)
        grad_up_ref[0, :, cols], grad_up_ref[1, :, cols] = halves_of(0, LATE_SLOTS + n)
        grad_up_ref[2, :, cols], down_o_ref[:, cols] = halves_of(1, LATE_SLOTS + n)
    for copy in copies:
        copy.wait()


def finish_part(summed, d_low, down):
    resident = pl.BlockSpec(memory_space=VMEM)
    return pl.pallas_call(
        finish_kernel,
        out_shape=(
            jax.ShapeDtypeStruct((1, TOKENS, MODEL), BF16),
            jax.ShapeDtypeStruct((3, RANK, MODEL), BF16),
            jax.ShapeDtypeStruct((3, RANK, HEADS_WIDTH), BF16),
            jax.ShapeDtypeStruct((RANK, HEADS_WIDTH), BF16),
            jax.ShapeDtypeStruct((RANK, MODEL), BF16),
        ),
        in_specs=[resident] * 3,
        out_specs=(pl.BlockSpec(memory_space=pl.ANY),) + (resident,) * 4,
        scratch_shapes=[VMEM((TOKENS, MODEL), BF16), DMA((4,))],
        compiler_params=pltpu.CompilerParams(vmem_limit_bytes=32 << 20),
    )(summed, d_low, down)


def per_device(hidden, projected, gradient, weight, down, up, down_o, up_o):
    down = down.reshape(3 * RANK, MODEL)
    d_low, summed = attention_part(hidden, projected, gradient, weight, down, up, down_o, up_o)
    return finish_part(summed, d_low, down)


def solution(mesh):
    in_specs = (
        P("dp", "ctx", None),
        P(None, "dp", "ctx", None),
        P("dp", "ctx", None),
        P(),
        P(),
        P(),
        P(),
        P(),
    )
    out_specs = (P("dp", "ctx", None), P(), P(), P(), P())
    return jax.shard_map(
        per_device, mesh=mesh, in_specs=in_specs, out_specs=out_specs, check_vma=False
    )
```

time: 69.2 us -> 67.2 us (0.971)
  Pallas kernels: 66.5 us -> 64.6 us
    pallas_call x1 -> x0, Pallas kernels: 24.8 us -> none  [reduce_part(): pl.pallas_call(reduce_kernel, out_shape=jax.ShapeDtypeStruct((2, PLANE, 1...]
    pallas_call x1, Pallas kernels: 39.6 us -> 62.2 us  [attention_part(): pl.pallas_call(attention_kernel, out_shape=(jax.ShapeDtypeStruct((3 * RAN...]
where the time goes in v2:
time: 67.2 us; the launch traced here: 67 us
  Pallas kernels  64.6 us (96%)
  local copies, waits for them, and re-layouts  1.7 us (3%)
    pallas_call x1, Pallas kernels, attention_part(): pl.pallas_call(attention_kernel, out_shape=(jax.ShapeDtypeStruct((3 * RAN...  62.2 us
    pallas_call x1, Pallas kernels, finish_part(): pl.pallas_call(finish_kernel, out_shape=(jax.ShapeDtypeStruct((1, TOKENS,...  2.4 us
    unnamed x6, local copies, waits for them, and re-layouts  1.7 us

profile of v2, /device:TPU:1, one launch (start us, length us, event | category | flops | bytes accessed | tf_op | source)
XLA Modules:
  0.0 67.0 jit_solution(6453751299888016822)
XLA Ops:
  0.6 0.0 copy-start
  0.6 62.2 %shard_map.119 = (bf16[24,256]{1,0:T(8,128)(2,1)}, bf16[2,48,16,128]{3,2,1,0:T(8,128)(2,1)}) custom-call(bf16[1,256,4096]{2,1,0:T(8,128)(2,1)} %hidden_hbm.1, bf16[3,1,256,2048]{3,2,1,0:T(8,128)(2,1)} %projected_hbm.1, bf16[1,256,4096]{2,1,0:T(8,128)(2,1)} %gradient_hbm.1, bf16[2048,4096]{1,0:T(8,128)(2,1)} %weight_hbm.1, bf16[24,4096]{1,0:T(8,128)(2,1)} %bitcast.1, ...), custom_call_target="tpu_custom_call" | custom-call | tf_op jit(solution)/shard_map/pallas_call | solution.py:433
  62.9 0.0 copy-done
  62.9 0.0 copy-start.1
  62.9 1.0 %copy-done.1 = bf16[2,48,16,128]{3,2,1,0:T(8,128)(2,1)S(1)} copy-done((bf16[2,48,16,128]{3,2,1,0:T(8,128)(2,1)S(1)}, bf16[2,48,16,128]{3,2,1,0:T(8,128)(2,1)}, u32[]{:S(2)}) %copy-start.1) | copy-done | bytes 393240
  63.9 0.0 copy-start.2
  63.9 0.7 %copy-done.2 = bf16[24,256]{1,0:T(8,128)(2,1)S(1)} copy-done((bf16[24,256]{1,0:T(8,128)(2,1)S(1)}, bf16[24,256]{1,0:T(8,128)(2,1)}, u32[]{:S(2)}) %copy-start.2) | copy-done | bytes 12312
  64.6 2.4 %shard_map.120 = (bf16[1,256,4096]{2,1,0:T(8,128)(2,1)}, bf16[3,8,4096]{2,1,0:T(8,128)(2,1)}, bf16[3,8,2048]{2,1,0:T(8,128)(2,1)}, bf16[8,2048]{1,0:T(8,128)(2,1)}, bf16[8,4096]{1,0:T(8,128)(2,1)}) custom-call(bf16[2,48,16,128]{3,2,1,0:T(8,128)(2,1)S(1)} %copy-done.1, bf16[24,256]{1,0:T(8,128)(2,1)S(1)} %copy-done.2, bf16[24,4096]{1,0:T(8,128)(2,1)S(1)} %bitcast.2), custom_call_target="tpu_custom_call" | custom-call | tf_op jit(solution)/shard_map/pallas_call | solution.py:522
Async XLA Ops:
  0.6 62.2 %copy-start = (bf16[3,8,4096]{2,1,0:T(8,128)(2,1)S(1)}, bf16[3,8,4096]{2,1,0:T(8,128)(2,1)}, u32[]{:S(2)}) copy-start(bf16[3,8,4096]{2,1,0:T(8,128)(2,1)} %param.12) | copy-start | bytes 589828
  62.9 1.0 %copy-start.1 = (bf16[2,48,16,128]{3,2,1,0:T(8,128)(2,1)S(1)}, bf16[2,48,16,128]{3,2,1,0:T(8,128)(2,1)}, u32[]{:S(2)}) copy-start(bf16[2,48,16,128]{3,2,1,0:T(8,128)(2,1)} %get-tuple-element.7.summed_ref) | copy-start | bytes 1179652
  63.9 0.7 %copy-start.2 = (bf16[24,256]{1,0:T(8,128)(2,1)S(1)}, bf16[24,256]{1,0:T(8,128)(2,1)}, u32[]{:S(2)}) copy-start(bf16[24,256]{1,0:T(8,128)(2,1)} %get-tuple-element.8.d_low_ref) | copy-start | bytes 36868

commit v3 on v2

v3 whole, which is shorter than its diff:
```python
import functools
import math

import jax
import jax.numpy as jnp
from jax import lax
from jax.experimental import pallas as pl
from jax.experimental.pallas import tpu as pltpu
from jax.sharding import PartitionSpec as P

MESH = pl.DeviceIdType.MESH
DMA = pltpu.SemaphoreType.DMA
VMEM = pltpu.VMEM
F32 = jnp.float32
BF16 = jnp.bfloat16

TOKENS = 256
MODEL = 4096
HEADS_WIDTH = 2048
HALF = 1024
HEAD = 128
RANK = 8
CTX = 32
SCALE = 1.0 / math.sqrt(HEAD)
EXP2_SCALE = SCALE * math.log2(math.e)
GRAD_SCALE = 2.0 / 32768
OW_BLOCK = 512

TILE = 128
LATE_SLOTS = 32
SLOTS = 48
AHEAD = 768
BACK = 256
FIRST_STEP = 2
DEVICES = 128


def nn(a, b):
    return lax.dot_general(a, b, (((1,), (0,)), ((), ())), preferred_element_type=F32)


def nt(a, b):
    return lax.dot_general(a, b, (((1,), (1,)), ((), ())), preferred_element_type=F32)


def tn(a, b):
    return lax.dot_general(a, b, (((0,), (0,)), ((), ())), preferred_element_type=F32)


def lanes(start, size):
    return pl.ds(pl.multiple_of(start, 128), size)


def stacked(top, bottom):
    return jnp.concatenate([top, bottom], axis=0).astype(BF16)


def tile_of(value, n):
    return value[:, n * TILE : (n + 1) * TILE]


def attention_kernel(
    hidden_hbm,
    projected_hbm,
    gradient_hbm,
    weight_hbm,
    down_ref,
    up_ref,
    down_o_ref,
    up_o_ref,
    d_low_ref,
    summed_ref,
    hid,
    q,
    k,
    v,
    og,
    ow,
    far_k,
    far_v,
    next_qkv,
    next_d,
    d_attn,
    att,
    dq,
    dk,
    dv,
    dk_far,
    dv_far,
    next_att,
    next_dq,
    next_dk,
    next_dv,
    dk_cross,
    dv_cross,
    thin,
    far_low,
    next_thin,
    totals,
    far_send,
    far_recv,
    next_send,
    next_recv,
    low,
    parts,
    in_sem,
    ow_sem,
    qkv_sem,
    kv_send_sem,
    kv_recv_sem,
    back_send_sem,
    back_recv_sem,
    small_send_sem,
    small_recv_sem,
    part_send_sem,
    part_recv_sem,
    sum_send_sem,
    sum_recv_sem,
    last_sems,
):
    dp = lax.axis_index("dp")
    ctx = lax.axis_index("ctx")
    following = (dp, lax.rem(ctx + 1, CTX))
    previous = (dp, lax.rem(ctx + CTX - 1, CTX))
    parity = lax.rem(ctx, 2)
    first_start = parity * HALF
    pair_start = (1 - parity) * HALF
    core = lax.rem(dp, 2)
    y_lo = dp // 2
    me = dp * CTX + ctx

    def remote(source, target, send_sem, recv_sem, device):
        return pltpu.make_async_remote_copy(
            src_ref=source,
            dst_ref=target,
            send_sem=send_sem,
            recv_sem=recv_sem,
            device_id=device,
            device_id_type=MESH,
        )

    def ow_copy(block):
        start = first_start if block < 2 else pair_start
        row = start + block % 2 * OW_BLOCK
        return pltpu.make_async_copy(
            weight_hbm.at[pl.ds(pl.multiple_of(row, OW_BLOCK), OW_BLOCK), :],
            ow.at[block * OW_BLOCK : (block + 1) * OW_BLOCK, :],
            ow_sem.at[block],
        )

    og_copy = pltpu.make_async_copy(gradient_hbm.at[0], og, in_sem.at[0])
    hid_copy = pltpu.make_async_copy(hidden_hbm.at[0], hid, in_sem.at[1])
    qkv_copies = [
        [
            pltpu.make_async_copy(
                projected_hbm.at[c, 0, :, lanes(start, HALF)],
                ref.at[:, at * HALF : (at + 1) * HALF],
                qkv_sem.at[at, c],
            )
            for c, ref in enumerate((q, k, v))
        ]
        for at, start in enumerate((first_start, pair_start))
    ]
    og_copy.start()
    ow_copy(3).start()

    barrier = pltpu.get_barrier_semaphore()

    def greet(n, carry):
        other = lax.rem(ctx + n, CTX)
        for other_dp in range(4):

            @pl.when(jnp.logical_or(n != 0, other_dp != dp))
            def _():
                pl.semaphore_signal(
                    barrier, inc=1, device_id=(other_dp, other), device_id_type=MESH
                )

        return carry

    lax.fori_loop(0, CTX, greet, 0)
    pl.semaphore_wait(barrier, DEVICES - 1)
    sent = []
    for j in range(3):
        for c, ref in ((0, far_k), (1, far_v)):
            copy = remote(
                projected_hbm.at[c + 1, 0, :, lanes(first_start + j * 256, 256)],
                ref.at[:, j * 256 : (j + 1) * 256],
                kv_send_sem.at[j, c],
                kv_recv_sem.at[j, c],
                following,
            )
            copy.start()
            sent.append(copy)
    back = [
        remote(
            projected_hbm.at[c, 0, :, lanes(pair_start + AHEAD, BACK)],
            next_qkv.at[c],
            back_send_sem.at[c],
            back_recv_sem.at[c],
            previous,
        )
        for c in range(3)
    ]
    for copy in back:
        copy.start()

    ow_copy(0).start()
    hid_copy.start()
    og_copy.wait()
    dy_low = nt(up_o_ref[...], og[...]).astype(BF16)

    def project(block):
        ow_copy(block).wait()
        start = first_start if block < 2 else pair_start
        column = start + block % 2 * OW_BLOCK
        rows = slice(block * OW_BLOCK, (block + 1) * OW_BLOCK)
        through_adapter = tn(down_o_ref[:, lanes(column, OW_BLOCK)], dy_low)
        d_attn[rows, :] = (nt(ow[rows, :], og[...]) + 2.0 * through_adapter).astype(BF16)

    ow_copy(1).start()
    project(3)
    d_copy = remote(
        d_attn.at[HALF + AHEAD : HEADS_WIDTH, :],
        next_d,
        back_send_sem.at[3],
        back_recv_sem.at[3],
        previous,
    )
    d_copy.start()
    back.append(d_copy)
    for copy in qkv_copies[0]:
        copy.start()
    ow_copy(2).start()
    for copy in qkv_copies[1]:
        copy.start()

    hid_copy.wait()
    low_in = nt(down_ref[...], hid[...]).astype(BF16)
    thin[...] = jnp.concatenate([dy_low, low_in], axis=0)
    thin_copies = [
        remote(thin, next_thin, small_send_sem.at[0], small_recv_sem.at[0], previous),
        remote(
            thin.at[2 * RANK :], far_low, small_send_sem.at[1], small_recv_sem.at[1], following
        ),
    ]
    for copy in thin_copies:
        copy.start()
    project(0)
    project(1)
    project(2)

    key_row = lax.broadcasted_iota(jnp.int32, (TOKENS, TOKENS), 0)
    query_column = lax.broadcasted_iota(jnp.int32, (TOKENS, TOKENS), 1)
    seen = key_row <= query_column

    def head(q_head, d_head, keys, values):
        scores = [nt(key, q_head) * EXP2_SCALE for key in keys]
        scores[0] = jnp.where(seen, scores[0], -jnp.inf)
        row_max = functools.reduce(
            jnp.maximum, [jnp.max(score, axis=0, keepdims=True) for score in scores]
        )
        raised = [jnp.exp2(score - row_max) for score in scores]
        total = sum(jnp.sum(r, axis=0, keepdims=True) for r in raised)
        inverse = 1.0 / total
        probs = [r * inverse for r in raised]
        probs_low = [p.astype(BF16) for p in probs]
        d_probs = [nn(value, d_head) for value in values]
        row_dot = sum(
            jnp.sum(p * d, axis=0, keepdims=True) for p, d in zip(probs, d_probs)
        )
        d_scores = [(p * (d - row_dot)).astype(BF16) for p, d in zip(probs, d_probs)]
        attended = sum(tn(value, p) for value, p in zip(values, probs_low)).astype(BF16)
        d_query = (sum(tn(key, s) for key, s in zip(keys, d_scores)) * SCALE).astype(BF16)
        d_keys = [(nn(s, q_head) * SCALE).astype(BF16) for s in d_scores]
        d_values = [nt(p, d_head).astype(BF16) for p in probs_low]
        return attended, d_query, d_keys, d_values

    for copy in qkv_copies[0]:
        copy.wait()

    def first_heads(j, carry):
        for i in range(FIRST_STEP):
            at = (j * FIRST_STEP + i) * HEAD
            cols, rows = lanes(at, HEAD), pl.ds(pl.multiple_of(at, HEAD), HEAD)
            att[rows, :], dq[rows, :], d_keys, d_values = head(
                q[:, cols], d_attn[rows, :], [k[:, cols]], [v[:, cols]]
            )
            dk[:, cols], dv[:, cols] = d_keys[0], d_values[0]
        return carry

    lax.fori_loop(0, 8 // FIRST_STEP, first_heads, 0)

    first = lanes(first_start, HALF)
    totals[:RANK] = nn(up_ref[0, :, first], dq[:HALF, :])
    totals[RANK : 2 * RANK] = nt(up_ref[1, :, first], dk[:, :HALF])
    totals[2 * RANK : 3 * RANK] = nt(up_ref[2, :, first], dv[:, :HALF])
    totals[3 * RANK :] = nn(down_o_ref[:, first], att[:HALF, :])
    first_slot = LATE_SLOTS + first_start // TILE
    pair_slot = LATE_SLOTS + pair_start // TILE

    def pack(slot, ups, down_o):
        for n in range(down_o.shape[1] // TILE):
            low[slot + n] = stacked(tile_of(ups[0], n), tile_of(ups[1], n))
            low[SLOTS + slot + n] = stacked(tile_of(ups[2], n), tile_of(down_o, n))

    def ups_of(low_in_all, rows, cols, d_query, d_key, d_value):
        return [
            nt(low_in_all[:RANK], d_query[rows, :]),
            nn(low_in_all[RANK : 2 * RANK], d_key[:, cols]),
            nn(low_in_all[2 * RANK :], d_value[:, cols]),
        ]

    ahead = slice(0, AHEAD)
    pack(first_slot, ups_of(low_in, ahead, ahead, dq, dk, dv), nt(dy_low, att[:AHEAD, :]))
    for n in (6, 7):
        low[pair_slot + n] = jnp.zeros((16, TILE), BF16)
        low[SLOTS + pair_slot + n] = jnp.zeros((16, TILE), BF16)

    for copy in qkv_copies[1]:
        copy.wait()

    def arrived(ref, sem):
        pltpu.make_async_copy(ref, ref, sem).wait()

    whole = slice(0, BACK)
    turned = lanes(first_start + AHEAD, BACK)

    def next_device_heads():
        for c in range(3):
            arrived(next_qkv.at[c], back_recv_sem.at[c])
        arrived(next_d, back_recv_sem.at[3])
        arrived(next_thin, small_recv_sem.at[0])
        for i in range(2):
            part = slice(i * HEAD, (i + 1) * HEAD)
            cols = slice(AHEAD + i * HEAD, AHEAD + (i + 1) * HEAD)
            next_att[part, :], next_dq[part, :], d_keys, d_values = head(
                next_qkv[0, :, part],
                next_d[part, :],
                [next_qkv[1, :, part], k[:, cols]],
                [next_qkv[2, :, part], v[:, cols]],
            )
            next_dk[:, part], dk_cross[:, part] = d_keys
            next_dv[:, part], dv_cross[:, part] = d_values
        next_send[:RANK] = nn(up_ref[0, :, turned], next_dq[...])
        next_send[RANK : 2 * RANK] = nt(up_ref[1, :, turned], next_dk[...])
        next_send[2 * RANK : 3 * RANK] = nt(up_ref[2, :, turned], next_dv[...])
        next_send[3 * RANK :] = nn(down_o_ref[:, turned], next_att[...])
        next_copy.start()
        totals[RANK : 2 * RANK] += nt(up_ref[1, :, turned], dk_cross[...])
        totals[2 * RANK : 3 * RANK] += nt(up_ref[2, :, turned], dv_cross[...])
        own = ups_of(
            low_in, slice(AHEAD, HALF), slice(AHEAD, HALF), dq, dk, dv
        )
        other = ups_of(next_thin[RANK:], whole, whole, next_dq, next_dk, next_dv)
        ups = [a + b for a, b in zip(own, other)]
        ups[1] += nn(low_in[RANK : 2 * RANK], dk_cross[...])
        ups[2] += nn(low_in[2 * RANK :], dv_cross[...])
        down_o = nt(dy_low, att[AHEAD:HALF, :]) + nt(next_thin[:RANK], next_att[...])
        pack(first_slot + 6, ups, down_o)

    next_copy = remote(
        next_send, next_recv, small_send_sem.at[3], small_recv_sem.at[3], following
    )

    def pair_heads(j, carry):
        @pl.when(j == 2)
        def _():
            next_device_heads()

        for c, ref in ((0, far_k), (1, far_v)):
            arrived(ref.at[:, lanes(j * 256, 256)], kv_recv_sem.at[j, c])
        for i in range(2):
            far_cols = lanes(j * 256 + i * HEAD, HEAD)
            at = HALF + j * 256 + i * HEAD
            cols, rows = lanes(at, HEAD), pl.ds(pl.multiple_of(at, HEAD), HEAD)
            att[rows, :], dq[rows, :], d_keys, d_values = head(
                q[:, cols],
                d_attn[rows, :],
                [k[:, cols], far_k[:, far_cols]],
                [v[:, cols], far_v[:, far_cols]],
            )
            dk[:, cols], dk_far[:, far_cols] = d_keys
            dv[:, cols], dv_far[:, far_cols] = d_values
        return carry

    lax.fori_loop(0, 3, pair_heads, 0)

    pair = lanes(pair_start, AHEAD)
    far_send[:RANK] = nt(up_ref[1, :, pair], dk_far[...])
    far_send[RANK:] = nt(up_ref[2, :, pair], dv_far[...])
    far_copy = remote(far_send, far_recv, small_send_sem.at[2], small_recv_sem.at[2], previous)
    far_copy.start()

    z_place = [lax.rem(ctx + 2 + n, 4) for n in range(4)]
    x_place = lax.rem(ctx // 4, 4)
    y_place = ctx // 16

    def send_tiles(kind, base, count, late):
        y_of = [lax.rem(z + kind + (0 if late else 1), 2) for z in z_place]

        def send(j, carry):
            line = lax.rem(x_place + 2 + j, 4) * 4
            if count == 32:
                line += lax.rem(y_place + 1 + j // 4, 2) * 16
            else:
                line += base % 32
            for z, to_y in zip(z_place, y_of):
                to = line + z
                to_dp = to_y * 2 + kind

                @pl.when(jnp.logical_or(to != ctx, to_dp != dp))
                def _():
                    remote(
                        low.at[kind * SLOTS + to + (0 if late else LATE_SLOTS)],
                        parts.at[me],
                        part_send_sem,
                        part_recv_sem,
                        (to_dp, to),
                    ).start()

            return carry

        lax.fori_loop(0, count // 4, send, 0)

    pair_rows = slice(HALF, HALF + AHEAD)
    arrived(next_recv, small_recv_sem.at[3])
    low_o = (
        totals[3 * RANK :]
        + next_recv[3 * RANK :]
        + nn(down_o_ref[:, pair], att[pair_rows, :])
    ).astype(BF16)
    up_o = nn(low_o, og[...])
    for n in range(16):
        low[SLOTS + 16 + n] = stacked(tile_of(up_o, n), tile_of(up_o, n + 16))
    send_tiles(1, 16, 16, True)

    arrived(far_low, small_recv_sem.at[1])
    ups = ups_of(low_in, pair_rows, pair_rows, dq, dk, dv)
    ups[1] += nn(far_low[:RANK], dk_far[...])
    ups[2] += nn(far_low[RANK:], dv_far[...])
    pack(pair_slot, ups, nt(dy_low, att[pair_rows, :]))
    send_tiles(0, 0, 16, False)
    send_tiles(1, 0, 16, False)

    d_low = totals[: 3 * RANK] + next_recv[: 3 * RANK]
    d_low += jnp.concatenate(
        [
            nn(up_ref[0, :, pair], dq[pair_rows, :]),
            nt(up_ref[1, :, pair], dk[:, pair_rows]),
            nt(up_ref[2, :, pair], dv[:, pair_rows]),
        ],
        axis=0,
    )
    arrived(far_recv, small_recv_sem.at[2])
    d_low += jnp.concatenate([jnp.zeros((RANK, TOKENS), F32), far_recv[...]], axis=0)
    d_low = d_low.astype(BF16)
    d_low_ref[...] = d_low
    down = nn(d_low, hid[...])
    third = down[2 * RANK :]
    for n in range(32):
        low[n] = tile_of(down[: 2 * RANK], n).astype(BF16)
    for n in range(16):
        low[SLOTS + n] = stacked(tile_of(third, n), tile_of(third, n + 16))
    send_tiles(0, 0, 32, True)
    send_tiles(1, 0, 16, True)

    is_late = lax.rem(ctx + core, 2) == y_lo
    is_owner = jnp.logical_or(is_late, ctx < 16)
    slot = jnp.where(is_late, ctx, LATE_SLOTS + ctx)

    @pl.when(is_owner)
    def _():
        parts[me] = low[core * SLOTS + slot]
        arrived(parts.at[0 : DEVICES - 1], part_recv_sem)

        def add(n, total):
            return total + parts[n].astype(F32)

        total = lax.fori_loop(0, DEVICES, add, jnp.zeros((16, TILE), F32), unroll=8)
        summed_ref[core, slot] = (total * GRAD_SCALE).astype(BF16)

        def spread(j, carry):
            line = lax.rem(x_place + 2 + j, 4) * 4 + lax.rem(y_place + 1 + j // 4 % 2, 2) * 16
            to_y = lax.rem(y_lo + 1 + j // 8, 2)
            for z in z_place:
                to = line + z

                @pl.when(jnp.logical_or(to != ctx, to_y != y_lo))
                def _():
                    remote(
                        summed_ref.at[core, slot],
                        summed_ref.at[core, slot],
                        sum_send_sem,
                        sum_recv_sem,
                        (to_y * 2 + core, to),
                    ).start()

            return carry

        lax.fori_loop(0, 16, spread, 0)
        arrived(parts.at[0 : SLOTS - 1], sum_recv_sem)

    @pl.when(jnp.logical_not(is_owner))
    def _():
        arrived(parts.at[0:SLOTS], sum_recv_sem)

    last = remote(
        summed_ref.at[core],
        summed_ref.at[core],
        last_sems.at[0],
        last_sems.at[1],
        (y_lo * 2 + 1 - core, ctx),
    )
    last.start()

    @pl.when(is_owner)
    def _():
        arrived(low.at[0 : 2 * SLOTS - 1], part_send_sem)
        arrived(low.at[0:63], sum_send_sem)

    @pl.when(jnp.logical_not(is_owner))
    def _():
        arrived(low, part_send_sem)

    for copy in sent + back + thin_copies + [far_copy, next_copy]:
        copy.wait_send()
    last.wait()


def attention_part(hidden, projected, gradient, weight, down, up, down_o, up_o):
    ahead = VMEM((TOKENS, AHEAD), BF16)
    square = VMEM((TOKENS, BACK), BF16)
    whole = VMEM((TOKENS, HEADS_WIDTH), BF16)
    flipped = VMEM((HEADS_WIDTH, TOKENS), BF16)
    wide = VMEM((TOKENS, MODEL), BF16)
    anywhere = pl.BlockSpec(memory_space=pl.ANY)
    resident = pl.BlockSpec(memory_space=VMEM)
    return pl.pallas_call(
        attention_kernel,
        out_shape=(
            jax.ShapeDtypeStruct((3 * RANK, TOKENS), BF16),
            jax.ShapeDtypeStruct((2, SLOTS, 16, TILE), BF16),
        ),
        in_specs=[anywhere] * 4 + [resident] * 4,
        out_specs=(resident, resident),
        scratch_shapes=[
            wide,
            whole,
            whole,
            whole,
            wide,
            VMEM((HEADS_WIDTH, MODEL), BF16),
            ahead,
            ahead,
            VMEM((3, TOKENS, BACK), BF16),
            square,
            flipped,
            flipped,
            flipped,
            whole,
            whole,
            ahead,
            ahead,
            square,
            square,
            square,
            square,
            square,
            square,
            VMEM((4 * RANK, TOKENS), BF16),
            VMEM((2 * RANK, TOKENS), BF16),
            VMEM((4 * RANK, TOKENS), BF16),
            VMEM((4 * RANK, TOKENS), F32),
            VMEM((2 * RANK, TOKENS), F32),
            VMEM((2 * RANK, TOKENS), F32),
            VMEM((4 * RANK, TOKENS), F32),
            VMEM((4 * RANK, TOKENS), F32),
            VMEM((2 * SLOTS, 16, TILE), BF16),
            VMEM((DEVICES, 16, TILE), BF16),
            DMA((2,)),
            DMA((4,)),
            DMA((2, 3)),
            DMA((3, 2)),
            DMA((3, 2)),
            DMA((4,)),
            DMA((4,)),
            DMA((4,)),
            DMA((4,)),
            DMA,
            DMA,
            DMA,
            DMA,
            DMA((2,)),
        ],
        compiler_params=pltpu.CompilerParams(
            collective_id=0, has_side_effects=True, vmem_limit_bytes=56 << 20
        ),
    )(hidden, projected, gradient, weight, down, up, down_o, up_o)


def finish_kernel(
    summed_hbm,
    d_low_hbm,
    down_hbm,
    input_hbm,
    grad_down_ref,
    grad_up_ref,
    down_o_ref,
    up_o_ref,
    summed,
    d_low,
    down,
    result,
    in_sems,
    sems,
):
    fetches = [
        pltpu.make_async_copy(source, target, in_sems.at[n])
        for n, (source, target) in enumerate(
            ((d_low_hbm, d_low), (down_hbm, down), (summed_hbm, summed))
        )
    ]
    for fetch in fetches:
        fetch.start()
    fetches[0].wait()
    fetches[1].wait()
    copies = []
    for n in range(4):
        rows = slice(n * 64, (n + 1) * 64)
        result[rows, :] = (2.0 * tn(d_low[:, rows], down[...])).astype(BF16)
        copy = pltpu.make_async_copy(result.at[rows, :], input_hbm.at[0, rows, :], sems.at[n])
        copy.start()
        copies.append(copy)
    fetches[2].wait()

    def halves_of(kind, slot):
        tile = summed[kind, slot].astype(F32)
        return tile[:RANK].astype(BF16), tile[RANK:].astype(BF16)

    for n in range(32):
        cols = slice(n * TILE, (n + 1) * TILE)
        grad_down_ref[0, :, cols], grad_down_ref[1, :, cols] = halves_of(0, n)
    for n in range(16):
        cols = slice(n * TILE, (n + 1) * TILE)
        later = slice(HEADS_WIDTH + n * TILE, HEADS_WIDTH + (n + 1) * TILE)
        grad_down_ref[2, :, cols], grad_down_ref[2, :, later] = halves_of(1, n)
        up_o_ref[:, cols], up_o_ref[:, later] = halves_of(1, 16 + n)
        grad_up_ref[0, :, cols], grad_up_ref[1, :, cols] = halves_of(0, LATE_SLOTS + n)
        grad_up_ref[2, :, cols], down_o_ref[:, cols] = halves_of(1, LATE_SLOTS + n)
    for copy in copies:
        copy.wait()


def finish_part(summed, d_low, down):
    resident = pl.BlockSpec(memory_space=VMEM)
    anywhere = pl.BlockSpec(memory_space=pl.ANY)
    return pl.pallas_call(
        finish_kernel,
        out_shape=(
            jax.ShapeDtypeStruct((1, TOKENS, MODEL), BF16),
            jax.ShapeDtypeStruct((3, RANK, MODEL), BF16),
            jax.ShapeDtypeStruct((3, RANK, HEADS_WIDTH), BF16),
            jax.ShapeDtypeStruct((RANK, HEADS_WIDTH), BF16),
            jax.ShapeDtypeStruct((RANK, MODEL), BF16),
        ),
        in_specs=[anywhere] * 3,
        out_specs=(anywhere,) + (resident,) * 4,
        scratch_shapes=[
            VMEM((2, SLOTS, 16, TILE), BF16),
            VMEM((3 * RANK, TOKENS), BF16),
            VMEM((3 * RANK, MODEL), BF16),
            VMEM((TOKENS, MODEL), BF16),
            DMA((3,)),
            DMA((4,)),
        ],
        compiler_params=pltpu.CompilerParams(vmem_limit_bytes=60 << 20),
    )(summed, d_low, down)


def per_device(hidden, projected, gradient, weight, down, up, down_o, up_o):
    down = down.reshape(3 * RANK, MODEL)
    d_low, summed = attention_part(hidden, projected, gradient, weight, down, up, down_o, up_o)
    return finish_part(summed, d_low, down)


def solution(mesh):
    in_specs = (
        P("dp", "ctx", None),
        P(None, "dp", "ctx", None),
        P("dp", "ctx", None),
        P(),
        P(),
        P(),
        P(),
        P(),
    )
    out_specs = (P("dp", "ctx", None), P(), P(), P(), P())
    return jax.shard_map(
        per_device, mesh=mesh, in_specs=in_specs, out_specs=out_specs, check_vma=False
    )
```

time: 67.2 us -> 59.3 us (0.88)
  Pallas kernels: 64.6 us -> 58.5 us
  local copies, waits for them, and re-layouts: 1.7 us -> 0 us
    pallas_call x1, Pallas kernels: 62.2 us -> 55.1 us  [attention_part(): pl.pallas_call(attention_kernel, out_shape=(jax.ShapeDtypeStruct((3 * RAN...]
    unnamed x6 -> x0, local copies, waits for them, and re-layouts: 1.7 us -> none
    pallas_call x1, Pallas kernels: 2.4 us -> 3.37 us  [finish_part(): pl.pallas_call(finish_kernel, out_shape=(jax.ShapeDtypeStruct((1, TOKENS,...]
where the time goes in v3:
time: 59.3 us; the launch traced here: 59.1 us
  Pallas kernels  58.5 us (99%)
  between operations  0.64 us (1%)
    pallas_call x1, Pallas kernels, attention_part(): pl.pallas_call(attention_kernel, out_shape=(jax.ShapeDtypeStruct((3 * RAN...  55.1 us
    pallas_call x1, Pallas kernels, finish_part(): pl.pallas_call(finish_kernel, out_shape=(jax.ShapeDtypeStruct((1, TOKENS,...  3.37 us

profile of v3, /device:TPU:1, one launch (start us, length us, event | category | flops | bytes accessed | tf_op | source)
XLA Modules:
  0.0 59.1 jit_solution(16185402907906598337)
XLA Ops:
  0.6 55.1 %shard_map.119 = (bf16[24,256]{1,0:T(8,128)(2,1)}, bf16[2,48,16,128]{3,2,1,0:T(8,128)(2,1)}) custom-call(bf16[1,256,4096]{2,1,0:T(8,128)(2,1)} %hidden_hbm.1, bf16[3,1,256,2048]{3,2,1,0:T(8,128)(2,1)} %projected_hbm.1, bf16[1,256,4096]{2,1,0:T(8,128)(2,1)} %gradient_hbm.1, bf16[2048,4096]{1,0:T(8,128)(2,1)} %weight_hbm.1, bf16[24,4096]{1,0:T(8,128)(2,1)} %bitcast.1, ...), custom_call_target="tpu_custom_call" | custom-call | tf_op jit(solution)/shard_map/pallas_call | solution.py:539
  55.7 3.4 %shard_map.120 = (bf16[1,256,4096]{2,1,0:T(8,128)(2,1)}, bf16[3,8,4096]{2,1,0:T(8,128)(2,1)}, bf16[3,8,2048]{2,1,0:T(8,128)(2,1)}, bf16[8,2048]{1,0:T(8,128)(2,1)}, bf16[8,4096]{1,0:T(8,128)(2,1)}) custom-call(bf16[2,48,16,128]{3,2,1,0:T(8,128)(2,1)} %get-tuple-element.7.summed_hbm, bf16[24,256]{1,0:T(8,128)(2,1)} %get-tuple-element.8.d_low_hbm, ...), custom_call_target="tpu_custom_call" | custom-call | tf_op jit(solution)/shard_map/pallas_call | solution.py:658

commit v4 on v3

--- a/solution.py
+++ b/solution.py
@@ -33,6 +33,7 @@
 BACK = 256
 FIRST_STEP = 2
 DEVICES = 128
+CHIPS = 64
 
 
 def nn(a, b):
@@ -117,6 +118,8 @@
     sum_send_sem,
     sum_recv_sem,
     last_sems,
+    sibling,
+    sibling_sems,
 ):
     dp = lax.axis_index("dp")
     ctx = lax.axis_index("ctx")
@@ -396,27 +399,46 @@
     x_place = lax.rem(ctx // 4, 4)
     y_place = ctx // 16
 
-    def send_tiles(kind, base, count, late):
-        y_of = [lax.rem(z + kind + (0 if late else 1), 2) for z in z_place]
+    other_core = (y_lo * 2 + 1 - core, ctx)
+    chip = ctx * 2 + y_lo
+    mine = core * SLOTS
+    theirs = (1 - core) * SLOTS
+
+    def to_sibling(start, count, n):
+        return remote(
+            low.at[pl.ds(theirs + start, count)],
+            sibling.at[start : start + count],
+            sibling_sems.at[n, 0],
+            sibling_sems.at[n, 1],
+            other_core,
+        )
+
+    def add_sibling(start, count):
+        def add(n, carry):
+            at = start + n
+            low[mine + at] = (low[mine + at].astype(F32) + sibling[at].astype(F32)).astype(BF16)
+            return carry
+
+        lax.fori_loop(0, count, add, 0, unroll=8)
+
+    def send_tiles(count, late):
+        y_of = [lax.rem(z + core + (0 if late else 1), 2) for z in z_place]
 
         def send(j, carry):
             line = lax.rem(x_place + 2 + j, 4) * 4
             if count == 32:
                 line += lax.rem(y_place + 1 + j // 4, 2) * 16
-            else:
-                line += base % 32
             for z, to_y in zip(z_place, y_of):
                 to = line + z
-                to_dp = to_y * 2 + kind
-
-                @pl.when(jnp.logical_or(to != ctx, to_dp != dp))
+
+                @pl.when(jnp.logical_or(to != ctx, to_y != y_lo))
                 def _():
                     remote(
-                        low.at[kind * SLOTS + to + (0 if late else LATE_SLOTS)],
-                        parts.at[me],
+                        low.at[mine + to + (0 if late else LATE_SLOTS)],
+                        parts.at[chip],
                         part_send_sem,
                         part_recv_sem,
-                        (to_dp, to),
+                        (to_y * 2 + core, to),
                     ).start()
 
             return carry
@@ -433,15 +455,14 @@
     up_o = nn(low_o, og[...])
     for n in range(16):
         low[SLOTS + 16 + n] = stacked(tile_of(up_o, n), tile_of(up_o, n + 16))
-    send_tiles(1, 16, 16, True)
 
     arrived(far_low, small_recv_sem.at[1])
     ups = ups_of(low_in, pair_rows, pair_rows, dq, dk, dv)
     ups[1] += nn(far_low[:RANK], dk_far[...])
     ups[2] += nn(far_low[RANK:], dv_far[...])
     pack(pair_slot, ups, nt(dy_low, att[pair_rows, :]))
-    send_tiles(0, 0, 16, False)
-    send_tiles(1, 0, 16, False)
+    early_copy = to_sibling(LATE_SLOTS, 16, 0)
+    early_copy.start()
 
     d_low = totals[: 3 * RANK] + next_recv[: 3 * RANK]
     d_low += jnp.concatenate(
@@ -462,8 +483,14 @@
         low[n] = tile_of(down[: 2 * RANK], n).astype(BF16)
     for n in range(16):
         low[SLOTS + n] = stacked(tile_of(third, n), tile_of(third, n + 16))
-    send_tiles(0, 0, 32, True)
-    send_tiles(1, 0, 16, True)
+    late_copy = to_sibling(0, LATE_SLOTS, 1)
+    late_copy.start()
+    arrived(sibling.at[LATE_SLOTS:SLOTS], sibling_sems.at[0, 1])
+    add_sibling(LATE_SLOTS, 16)
+    arrived(sibling.at[0:LATE_SLOTS], sibling_sems.at[1, 1])
+    add_sibling(0, LATE_SLOTS)
+    send_tiles(32, True)
+    send_tiles(16, False)
 
     is_late = lax.rem(ctx + core, 2) == y_lo
     is_owner = jnp.logical_or(is_late, ctx < 16)
@@ -471,13 +498,13 @@
 
     @pl.when(is_owner)
     def _():
-        parts[me] = low[core * SLOTS + slot]
-        arrived(parts.at[0 : DEVICES - 1], part_recv_sem)
+        parts[chip] = low[mine + slot]
+        arrived(parts.at[0 : CHIPS - 1], part_recv_sem)
 
         def add(n, total):
             return total + parts[n].astype(F32)
 
-        total = lax.fori_loop(0, DEVICES, add, jnp.zeros((16, TILE), F32), unroll=8)
+        total = lax.fori_loop(0, CHIPS, add, jnp.zeros((16, TILE), F32), unroll=8)
         summed_ref[core, slot] = (total * GRAD_SCALE).astype(BF16)
 
         def spread(j, carry):
@@ -510,20 +537,20 @@
         summed_ref.at[core],
         last_sems.at[0],
         last_sems.at[1],
-        (y_lo * 2 + 1 - core, ctx),
+        other_core,
     )
     last.start()
 
     @pl.when(is_owner)
     def _():
-        arrived(low.at[0 : 2 * SLOTS - 1], part_send_sem)
+        arrived(low.at[0 : SLOTS - 1], part_send_sem)
         arrived(low.at[0:63], sum_send_sem)
 
     @pl.when(jnp.logical_not(is_owner))
     def _():
-        arrived(low, part_send_sem)
-
-    for copy in sent + back + thin_copies + [far_copy, next_copy]:
+        arrived(low.at[0:SLOTS], part_send_sem)
+
+    for copy in sent + back + thin_copies + [far_copy, next_copy, early_copy, late_copy]:
         copy.wait_send()
     last.wait()
 
@@ -577,7 +604,7 @@
             VMEM((4 * RANK, TOKENS), F32),
             VMEM((4 * RANK, TOKENS), F32),
             VMEM((2 * SLOTS, 16, TILE), BF16),
-            VMEM((DEVICES, 16, TILE), BF16),
+            VMEM((CHIPS, 16, TILE), BF16),
             DMA((2,)),
             DMA((4,)),
             DMA((2, 3)),
@@ -592,6 +619,8 @@
             DMA,
             DMA,
             DMA((2,)),
+            VMEM((SLOTS, 16, TILE), BF16),
+            DMA((2, 2)),
         ],
         compiler_params=pltpu.CompilerParams(
             collective_id=0, has_side_effects=True, vmem_limit_bytes=56 << 20

time: 59.3 us -> 59 us (level)
  no operation moved by 1% of the time
where the time goes in v4:
time: 59 us; the launch traced here: 58.9 us
  Pallas kernels  58.2 us (99%)
  between operations  0.64 us (1%)
    pallas_call x1, Pallas kernels, attention_part(): pl.pallas_call(attention_kernel, out_shape=(jax.ShapeDtypeStruct((3 * RAN...  54.8 us
    pallas_call x1, Pallas kernels, finish_part(): pl.pallas_call(finish_kernel, out_shape=(jax.ShapeDtypeStruct((1, TOKENS,...  3.38 us

profile of v4, /device:TPU:1, one launch (start us, length us, event | category | flops | bytes accessed | tf_op | source)
XLA Modules:
  0.0 58.9 jit_solution(2243904521681126386)
XLA Ops:
  0.6 54.8 %shard_map.119 = (bf16[24,256]{1,0:T(8,128)(2,1)}, bf16[2,48,16,128]{3,2,1,0:T(8,128)(2,1)}) custom-call(bf16[1,256,4096]{2,1,0:T(8,128)(2,1)} %hidden_hbm.1, bf16[3,1,256,2048]{3,2,1,0:T(8,128)(2,1)} %projected_hbm.1, bf16[1,256,4096]{2,1,0:T(8,128)(2,1)} %gradient_hbm.1, bf16[2048,4096]{1,0:T(8,128)(2,1)} %weight_hbm.1, bf16[24,4096]{1,0:T(8,128)(2,1)} %bitcast.1, ...), custom_call_target="tpu_custom_call" | custom-call | tf_op jit(solution)/shard_map/pallas_call | solution.py:566
  55.5 3.4 %shard_map.120 = (bf16[1,256,4096]{2,1,0:T(8,128)(2,1)}, bf16[3,8,4096]{2,1,0:T(8,128)(2,1)}, bf16[3,8,2048]{2,1,0:T(8,128)(2,1)}, bf16[8,2048]{1,0:T(8,128)(2,1)}, bf16[8,4096]{1,0:T(8,128)(2,1)}) custom-call(bf16[2,48,16,128]{3,2,1,0:T(8,128)(2,1)} %get-tuple-element.7.summed_hbm, bf16[24,256]{1,0:T(8,128)(2,1)} %get-tuple-element.8.d_low_hbm, ...), custom_call_target="tpu_custom_call" | custom-call | tf_op jit(solution)/shard_map/pallas_call | solution.py:687

commit v5 on v4

--- a/solution.py
+++ b/solution.py
@@ -69,7 +69,7 @@
     up_ref,
     down_o_ref,
     up_o_ref,
-    d_low_ref,
+    result_hbm,
     summed_ref,
     hid,
     q,
@@ -120,6 +120,8 @@
     last_sems,
     sibling,
     sibling_sems,
+    result,
+    result_sems,
 ):
     dp = lax.axis_index("dp")
     ctx = lax.axis_index("ctx")
@@ -476,7 +478,6 @@
     arrived(far_recv, small_recv_sem.at[2])
     d_low += jnp.concatenate([jnp.zeros((RANK, TOKENS), F32), far_recv[...]], axis=0)
     d_low = d_low.astype(BF16)
-    d_low_ref[...] = d_low
     down = nn(d_low, hid[...])
     third = down[2 * RANK :]
     for n in range(32):
@@ -492,6 +493,14 @@
     send_tiles(32, True)
     send_tiles(16, False)
 
+    result_copies = []
+    for n in range(4):
+        cols = slice(n * HALF, (n + 1) * HALF)
+        result[:, cols] = (2.0 * tn(d_low, down_ref[:, cols])).astype(BF16)
+        copy = pltpu.make_async_copy(result.at[:, cols], result_hbm.at[:, cols], result_sems.at[n])
+        copy.start()
+        result_copies.append(copy)
+
     is_late = lax.rem(ctx + core, 2) == y_lo
     is_owner = jnp.logical_or(is_late, ctx < 16)
     slot = jnp.where(is_late, ctx, LATE_SLOTS + ctx)
@@ -552,6 +561,8 @@
 
     for copy in sent + back + thin_copies + [far_copy, next_copy, early_copy, late_copy]:
         copy.wait_send()
+    for copy in result_copies:
+        copy.wait()
     last.wait()
 
 
@@ -566,11 +577,11 @@
     return pl.pallas_call(
         attention_kernel,
         out_shape=(
-            jax.ShapeDtypeStruct((3 * RANK, TOKENS), BF16),
+            jax.ShapeDtypeStruct((TOKENS, MODEL), BF16),
             jax.ShapeDtypeStruct((2, SLOTS, 16, TILE), BF16),
         ),
         in_specs=[anywhere] * 4 + [resident] * 4,
-        out_specs=(resident, resident),
+        out_specs=(anywhere, resident),
         scratch_shapes=[
             wide,
             whole,
@@ -621,6 +632,8 @@
             DMA((2,)),
             VMEM((SLOTS, 16, TILE), BF16),
             DMA((2, 2)),
+            wide,
+            DMA((4,)),
         ],
         compiler_params=pltpu.CompilerParams(
             collective_id=0, has_side_effects=True, vmem_limit_bytes=56 << 20
@@ -630,59 +643,77 @@
 
 def finish_kernel(
     summed_hbm,
-    d_low_hbm,
-    down_hbm,
+    result_hbm,
     input_hbm,
+    grad_down_hbm,
+    grad_up_hbm,
+    down_o_hbm,
+    up_o_hbm,
     grad_down_ref,
     grad_up_ref,
     down_o_ref,
     up_o_ref,
     summed,
-    d_low,
-    down,
     result,
+    fetch_sem,
     in_sems,
     sems,
+    out_sems,
 ):
+    fetch = pltpu.make_async_copy(summed_hbm, summed, fetch_sem)
+    fetch.start()
+    rows_of = [slice(n * 64, (n + 1) * 64) for n in range(4)]
     fetches = [
-        pltpu.make_async_copy(source, target, in_sems.at[n])
-        for n, (source, target) in enumerate(
-            ((d_low_hbm, d_low), (down_hbm, down), (summed_hbm, summed))
-        )
+        pltpu.make_async_copy(result_hbm.at[rows, :], result.at[rows, :], in_sems.at[n])
+        for n, rows in enumerate(rows_of)
     ]
-    for fetch in fetches:
-        fetch.start()
-    fetches[0].wait()
-    fetches[1].wait()
+    for copy in fetches:
+        copy.start()
+    fetch.wait()
+
+    def halves_of(kind, slot):
+        tile = summed[kind, slot].astype(F32)
+        return tile[:RANK].astype(BF16), tile[RANK:].astype(BF16)
+
     copies = []
-    for n in range(4):
-        rows = slice(n * 64, (n + 1) * 64)
-        result[rows, :] = (2.0 * tn(d_low[:, rows], down[...])).astype(BF16)
+
+    def pass_on(n):
+        fetches[n].wait()
+        rows = rows_of[n]
         copy = pltpu.make_async_copy(result.at[rows, :], input_hbm.at[0, rows, :], sems.at[n])
         copy.start()
         copies.append(copy)
-    fetches[2].wait()
-
-    def halves_of(kind, slot):
-        tile = summed[kind, slot].astype(F32)
-        return tile[:RANK].astype(BF16), tile[RANK:].astype(BF16)
-
-    for n in range(32):
-        cols = slice(n * TILE, (n + 1) * TILE)
-        grad_down_ref[0, :, cols], grad_down_ref[1, :, cols] = halves_of(0, n)
+
+    def send_out(source, target, n):
+        copy = pltpu.make_async_copy(source, target, out_sems.at[n])
+        copy.start()
+        copies.append(copy)
+
     for n in range(16):
         cols = slice(n * TILE, (n + 1) * TILE)
         later = slice(HEADS_WIDTH + n * TILE, HEADS_WIDTH + (n + 1) * TILE)
+        grad_down_ref[0, :, cols], grad_down_ref[1, :, cols] = halves_of(0, n)
+        grad_down_ref[0, :, later], grad_down_ref[1, :, later] = halves_of(0, 16 + n)
         grad_down_ref[2, :, cols], grad_down_ref[2, :, later] = halves_of(1, n)
+    send_out(grad_down_ref, grad_down_hbm, 0)
+    pass_on(0)
+    pass_on(1)
+    for n in range(16):
+        cols = slice(n * TILE, (n + 1) * TILE)
+        later = slice(HEADS_WIDTH + n * TILE, HEADS_WIDTH + (n + 1) * TILE)
         up_o_ref[:, cols], up_o_ref[:, later] = halves_of(1, 16 + n)
         grad_up_ref[0, :, cols], grad_up_ref[1, :, cols] = halves_of(0, LATE_SLOTS + n)
         grad_up_ref[2, :, cols], down_o_ref[:, cols] = halves_of(1, LATE_SLOTS + n)
+    send_out(grad_up_ref, grad_up_hbm, 1)
+    send_out(down_o_ref, down_o_hbm, 2)
+    send_out(up_o_ref, up_o_hbm, 3)
+    pass_on(2)
+    pass_on(3)
     for copy in copies:
         copy.wait()
 
 
-def finish_part(summed, d_low, down):
-    resident = pl.BlockSpec(memory_space=VMEM)
+def finish_part(summed, result):
     anywhere = pl.BlockSpec(memory_space=pl.ANY)
     return pl.pallas_call(
         finish_kernel,
@@ -693,24 +724,28 @@
             jax.ShapeDtypeStruct((RANK, HEADS_WIDTH), BF16),
             jax.ShapeDtypeStruct((RANK, MODEL), BF16),
         ),
-        in_specs=[anywhere] * 3,
-        out_specs=(anywhere,) + (resident,) * 4,
+        in_specs=[anywhere] * 2,
+        out_specs=(anywhere,) * 5,
         scratch_shapes=[
+            VMEM((3, RANK, MODEL), BF16),
+            VMEM((3, RANK, HEADS_WIDTH), BF16),
+            VMEM((RANK, HEADS_WIDTH), BF16),
+            VMEM((RANK, MODEL), BF16),
             VMEM((2, SLOTS, 16, TILE), BF16),
-            VMEM((3 * RANK, TOKENS), BF16),
-            VMEM((3 * RANK, MODEL), BF16),
             VMEM((TOKENS, MODEL), BF16),
-            DMA((3,)),
+            DMA,
+            DMA((4,)),
+            DMA((4,)),
             DMA((4,)),
         ],
         compiler_params=pltpu.CompilerParams(vmem_limit_bytes=60 << 20),
-    )(summed, d_low, down)
+    )(summed, result)
 
 
 def per_device(hidden, projected, gradient, weight, down, up, down_o, up_o):
     down = down.reshape(3 * RANK, MODEL)
-    d_low, summed = attention_part(hidden, projected, gradient, weight, down, up, down_o, up_o)
-    return finish_part(summed, d_low, down)
+    result, summed = attention_part(hidden, projected, gradient, weight, down, up, down_o, up_o)
+    return finish_part(summed, result)
 
 
 def solution(mesh):

time: 59 us -> 58.8 us (level)
  no operation moved by 1% of the time
where the time goes in v5:
time: 58.8 us; the launch traced here: 58.6 us
  Pallas kernels  58 us (99%)
  between operations  0.64 us (1%)
    pallas_call x1, Pallas kernels, attention_part(): pl.pallas_call(attention_kernel, out_shape=(jax.ShapeDtypeStruct((TOKENS,...  54.9 us
    pallas_call x1, Pallas kernels, finish_part(): pl.pallas_call(finish_kernel, out_shape=(jax.ShapeDtypeStruct((1, TOKENS,...  3.06 us

profile of v5, /device:TPU:1, one launch (start us, length us, event | category | flops | bytes accessed | tf_op | source)
XLA Modules:
  0.0 58.6 jit_solution(8585942624114347779)
XLA Ops:
  0.6 54.9 %shard_map.119 = (bf16[256,4096]{1,0:T(8,128)(2,1)}, bf16[2,48,16,128]{3,2,1,0:T(8,128)(2,1)}) custom-call(bf16[1,256,4096]{2,1,0:T(8,128)(2,1)} %hidden_hbm.1, bf16[3,1,256,2048]{3,2,1,0:T(8,128)(2,1)} %projected_hbm.1, bf16[1,256,4096]{2,1,0:T(8,128)(2,1)} %gradient_hbm.1, bf16[2048,4096]{1,0:T(8,128)(2,1)} %weight_hbm.1, bf16[24,4096]{1,0:T(8,128)(2,1)} %bitcast.1, ...), custom_call_target="tpu_custom_call" | custom-call | tf_op jit(solution)/shard_map/pallas_call | solution.py:577
  55.5 3.1 %shard_map.120 = (bf16[1,256,4096]{2,1,0:T(8,128)(2,1)}, bf16[3,8,4096]{2,1,0:T(8,128)(2,1)}, bf16[3,8,2048]{2,1,0:T(8,128)(2,1)}, bf16[8,2048]{1,0:T(8,128)(2,1)}, bf16[8,4096]{1,0:T(8,128)(2,1)}) custom-call(bf16[2,48,16,128]{3,2,1,0:T(8,128)(2,1)} %get-tuple-element.7.summed_hbm, bf16[256,4096]{1,0:T(8,128)(2,1)} %get-tuple-element.8.result_hbm), custom_call_target="tpu_custom_call" | custom-call | tf_op jit(solution)/shard_map/pallas_call | solution.py:718

commit v6 on v5

--- a/solution.py
+++ b/solution.py
@@ -31,7 +31,7 @@
 SLOTS = 48
 AHEAD = 768
 BACK = 256
-FIRST_STEP = 2
+FIRST_STEP = 4
 DEVICES = 128
 CHIPS = 64
 

time: 58.8 us -> 58.8 us (level)
  no operation moved by 1% of the time
where the time goes in v6:
time: 58.8 us; the launch traced here: 58.6 us
  Pallas kernels  58 us (99%)
  between operations  0.64 us (1%)
    pallas_call x1, Pallas kernels, attention_part(): pl.pallas_call(attention_kernel, out_shape=(jax.ShapeDtypeStruct((TOKENS,...  54.9 us
    pallas_call x1, Pallas kernels, finish_part(): pl.pallas_call(finish_kernel, out_shape=(jax.ShapeDtypeStruct((1, TOKENS,...  3.06 us

profile of v6, /device:TPU:1, one launch (start us, length us, event | category | flops | bytes accessed | tf_op | source)
XLA Modules:
  0.0 58.6 jit_solution(10798247702310247293)
XLA Ops:
  0.6 54.9 %shard_map.119 = (bf16[256,4096]{1,0:T(8,128)(2,1)}, bf16[2,48,16,128]{3,2,1,0:T(8,128)(2,1)}) custom-call(bf16[1,256,4096]{2,1,0:T(8,128)(2,1)} %hidden_hbm.1, bf16[3,1,256,2048]{3,2,1,0:T(8,128)(2,1)} %projected_hbm.1, bf16[1,256,4096]{2,1,0:T(8,128)(2,1)} %gradient_hbm.1, bf16[2048,4096]{1,0:T(8,128)(2,1)} %weight_hbm.1, bf16[24,4096]{1,0:T(8,128)(2,1)} %bitcast.1, ...), custom_call_target="tpu_custom_call" | custom-call | tf_op jit(solution)/shard_map/pallas_call | solution.py:577
  55.6 3.1 %shard_map.120 = (bf16[1,256,4096]{2,1,0:T(8,128)(2,1)}, bf16[3,8,4096]{2,1,0:T(8,128)(2,1)}, bf16[3,8,2048]{2,1,0:T(8,128)(2,1)}, bf16[8,2048]{1,0:T(8,128)(2,1)}, bf16[8,4096]{1,0:T(8,128)(2,1)}) custom-call(bf16[2,48,16,128]{3,2,1,0:T(8,128)(2,1)} %get-tuple-element.7.summed_hbm, bf16[256,4096]{1,0:T(8,128)(2,1)} %get-tuple-element.8.result_hbm), custom_call_target="tpu_custom_call" | custom-call | tf_op jit(solution)/shard_map/pallas_call | solution.py:718
